TPU v7x, 32 devices: a whole 2x2x4 slice. The times are simulated.
32 devices in a mesh: dp: 8 (over y, x, core), tp: 4 (over z).
Axes of the slice: x: 2, y: 2, z: 4, core: 2. Of those that a mesh axis runs over, the one named last changes fastest.
Arguments:
- rows_in: bfloat16 [8192, 1024], P(('dp', 'tp')), may hold values from -6 to 6
- memory: bfloat16 [4096, 1024], P(('dp', 'tp')), may hold values from -6 to 6
- lengths: int32 [8], P('dp'), may hold values from 256 to 1024, as said below
- mem_lengths: int32 [8], P('dp'), may hold values from 128 to 512, as said below
- cotangent: bfloat16 [8192, 1024], P(('dp', 'tp')), may hold values from -6 to 6
- query_w: float32 [1024, 1024], P('dp', 'tp'), may hold values from -0.1875 to 0.1875
- keyval_w: float32 [2, 1024, 512], P(None, 'dp', 'tp'), may hold values from -0.1875 to 0.1875
- out_w: float32 [1024, 1024], P('tp', 'dp'), may hold values from -2 to 2
- cross_query_w: float32 [1024, 1024], P('dp', 'tp'), may hold values from -0.1875 to 0.1875
- cross_keyval_w: float32 [2, 1024, 512], P(None, 'dp', 'tp'), may hold values from -0.1875 to 0.1875
- cross_out_w: float32 [1024, 1024], P('tp', 'dp'), may hold values from -1.5 to 1.5
- gateup_w: float32 [2, 1024, 2816], P(None, 'dp', 'tp'), may hold values from -0.1875 to 0.1875
- down_w: float32 [2816, 1024], P('tp', 'dp'), may hold values from -0.109375 to 0.109375
- gains: float32 [3, 1024], P(None, 'dp'), may hold values from 0.5 to 1.5
- rel_table: float32 [16, 32], P('tp', 'dp'), may hold values from -4 to 4
- query_m: float32 [1024, 1024], P('dp', 'tp'), may hold values from -0.0004272461 to 0.0004272461
- keyval_m: float32 [2, 1024, 512], P(None, 'dp', 'tp'), may hold values from -0.0004272461 to 0.0004272461
- out_m: float32 [1024, 1024], P('tp', 'dp'), may hold values from -0.00010681152 to 0.00010681152
- cross_query_m: float32 [1024, 1024], P('dp', 'tp'), may hold values from -0.0004272461 to 0.0004272461
- cross_keyval_m: float32 [2, 1024, 512], P(None, 'dp', 'tp'), may hold values from -0.0004272461 to 0.0004272461
- cross_out_m: float32 [1024, 1024], P('tp', 'dp'), may hold values from -7.6293945e-05 to 7.6293945e-05
- gateup_m: float32 [2, 1024, 2816], P(None, 'dp', 'tp'), may hold values from -0.00018310547 to 0.00018310547
- down_m: float32 [2816, 1024], P('tp', 'dp'), may hold values from -0.0004272461 to 0.0004272461
- gains_m: float32 [3, 1024], P(None, 'dp'), may hold values from -0.0017089844 to 0.0017089844
- rel_table_m: float32 [16, 32], P('tp', 'dp'), may hold values from -0.0017089844 to 0.0017089844
- query_v: float32 [1024, 1024], P('dp', 'tp'), may hold values from 3.5461487e-09 to 1.4050777e-08
- keyval_v: float32 [2, 1024, 512], P(None, 'dp', 'tp'), may hold values from 3.5461487e-09 to 1.4050777e-08
- out_v: float32 [1024, 1024], P('tp', 'dp'), may hold values from 2.141071e-10 to 8.4304663e-10
- cross_query_v: float32 [1024, 1024], P('dp', 'tp'), may hold values from 3.5461487e-09 to 1.4050777e-08
- cross_keyval_v: float32 [2, 1024, 512], P(None, 'dp', 'tp'), may hold values from 3.5461487e-09 to 1.4050777e-08
- cross_out_v: float32 [1024, 1024], P('tp', 'dp'), may hold values from 1.4050777e-10 to 5.620311e-10
- gateup_v: float32 [2, 1024, 2816], P(None, 'dp', 'tp'), may hold values from 7.0922973e-10 to 2.8101554e-09
- down_v: float32 [2816, 1024], P('tp', 'dp'), may hold values from 3.5461487e-09 to 1.4050777e-08
- gains_v: float32 [3, 1024], P(None, 'dp'), may hold values from 5.620311e-08 to 2.2748878e-07
- rel_table_v: float32 [16, 32], P('tp', 'dp'), may hold values from 5.620311e-08 to 2.2748878e-07
Outputs:
- block_out: bfloat16 [8192, 1024], P(('dp', 'tp'))
- grad_rows: float32 [8192, 1024], P(('dp', 'tp'))
- grad_memory: float32 [4096, 1024], P(('dp', 'tp'))
- grad_norm: float32 [], replicated
- new_query_m: float32 [1024, 1024], P('dp', 'tp')
- new_keyval_m: float32 [2, 1024, 512], P(None, 'dp', 'tp')
- new_out_m: float32 [1024, 1024], P('tp', 'dp')
- new_cross_query_m: float32 [1024, 1024], P('dp', 'tp')
- new_cross_keyval_m: float32 [2, 1024, 512], P(None, 'dp', 'tp')
- new_cross_out_m: float32 [1024, 1024], P('tp', 'dp')
- new_gateup_m: float32 [2, 1024, 2816], P(None, 'dp', 'tp')
- new_down_m: float32 [2816, 1024], P('tp', 'dp')
- new_gains_m: float32 [3, 1024], P(None, 'dp')
- new_rel_table_m: float32 [16, 32], P('tp', 'dp')
- new_query_v: float32 [1024, 1024], P('dp', 'tp')
- new_keyval_v: float32 [2, 1024, 512], P(None, 'dp', 'tp')
- new_out_v: float32 [1024, 1024], P('tp', 'dp')
- new_cross_query_v: float32 [1024, 1024], P('dp', 'tp')
- new_cross_keyval_v: float32 [2, 1024, 512], P(None, 'dp', 'tp')
- new_cross_out_v: float32 [1024, 1024], P('tp', 'dp')
- new_gateup_v: float32 [2, 1024, 2816], P(None, 'dp', 'tp')
- new_down_v: float32 [2816, 1024], P('tp', 'dp')
- new_gains_v: float32 [3, 1024], P(None, 'dp')
- new_rel_table_v: float32 [16, 32], P('tp', 'dp')
- new_query_w: float32 [1024, 1024], P('dp', 'tp')
- new_keyval_w: float32 [2, 1024, 512], P(None, 'dp', 'tp')
- new_out_w: float32 [1024, 1024], P('tp', 'dp')
- new_cross_query_w: float32 [1024, 1024], P('dp', 'tp')
- new_cross_keyval_w: float32 [2, 1024, 512], P(None, 'dp', 'tp')
- new_cross_out_w: float32 [1024, 1024], P('tp', 'dp')
- new_gateup_w: float32 [2, 1024, 2816], P(None, 'dp', 'tp')
- new_down_w: float32 [2816, 1024], P('tp', 'dp')
- new_gains: float32 [3, 1024], P(None, 'dp')
- new_rel_table: float32 [16, 32], P('tp', 'dp')
Inputs may be any that keep to these rules, and one draw needn't show every extreme that they name: `lengths`: exactly one of the 8 sequences has length 1024. `mem_lengths`: exactly one of the 8 sequences has 512 valid memory rows.
All inputs are finite; a program needn't handle non-finite values.
Results may differ from a plain program's by a relative error of at most 0.023.
Values may be sent and summed in bfloat16 or wider, within the bound.
A program may use at most 192 MiB of HBM per device.

v0:
```python
import math

import jax
import jax.numpy as jnp
import numpy as np
from jax import lax
from jax.sharding import PartitionSpec as P

D = 1024
H = 16
DH = 64
FF = 2816
SEQ_LEN = 1024
MEM = 512
STEP = 10


bucket_edges = np.array(
    [math.ceil(16.0 * 8.0 ** ((level - 16) / 16.0)) for level in range(17, 32)], dtype=np.int32
)
score_scale = 0.125
masked_fill = -1e30
norm_epsilon = 1e-06
clip_limit = 1.0
beta_one = 0.9
beta_two = 0.95
adam_epsilon = 1e-08
decay_rate = 0.1


def update_rates():
    return (
        D ** (-0.5),
        D ** (-0.5),
        max(1, H * DH * 8 // SEQ_LEN) ** (-0.5),
        D ** (-0.5),
        D ** (-0.5),
        max(1, H * DH * 8 // MEM) ** (-0.5),
        D ** (-0.5),
        FF ** (-0.5),
        1.0,
        0.5,
    )


def bucket_index(offset):
    passed = jnp.sum((offset[..., None] >= jnp.asarray(bucket_edges)).astype(jnp.int32), axis=-1)
    return jnp.where(offset < 16, offset, 16 + passed)


def bucket_onehot(seq_len, buckets):
    offsets = jnp.arange(seq_len, dtype=jnp.int32)
    levels = jnp.arange(buckets, dtype=jnp.int32)
    return (bucket_index(offsets)[:, None] == levels[None, :]).astype(jnp.float32)


def rms_scale(rows, gain):
    return rows * lax.rsqrt(jnp.mean(rows * rows, axis=-1, keepdims=True) + norm_epsilon) * gain


def gain_term(grad, rows):
    return jnp.sum(
        grad * rows * lax.rsqrt(jnp.mean(rows * rows, axis=-1, keepdims=True) + norm_epsilon),
        axis=0,
    )


def gelu_pair(gate_pre, up_part):
    return jax.nn.gelu(gate_pre, approximate=True) * up_part


def toeplitz_bias(bias_vec, row_start, block_rows):
    head_count = bias_vec.shape[0]
    key_len = bias_vec.shape[1]
    width = key_len + block_rows - 1
    padded = jnp.concatenate(
        [
            jnp.broadcast_to(bias_vec[:, :1], (head_count, key_len)),
            bias_vec,
            jnp.zeros((head_count, block_rows), jnp.float32),
        ],
        axis=1,
    )
    strip = lax.dynamic_slice_in_dim(padded, row_start + 1, width, 1)
    tiled = jnp.tile(strip, (1, block_rows + 1))[:, : block_rows * (width + 1)]
    shifted = tiled.reshape(head_count, block_rows, width + 1)[:, :, :key_len]
    return jnp.flip(shifted, axis=2)


def diagonal_sums(grads, row_start):
    head_count, block_rows, key_len = grads.shape
    flipped = jnp.flip(grads, axis=2)
    padded = jnp.concatenate(
        [flipped, jnp.zeros((head_count, block_rows, block_rows), jnp.float32)], axis=2
    )
    flat = padded.reshape(head_count, block_rows * (key_len + block_rows))[
        :, : block_rows * (key_len + block_rows - 1)
    ]
    column_sums = jnp.sum(flat.reshape(head_count, block_rows, key_len + block_rows - 1), axis=1)
    extended = jnp.concatenate([column_sums, jnp.zeros((head_count, key_len), jnp.float32)], axis=1)
    return lax.dynamic_slice_in_dim(extended, key_len - 1 - row_start, key_len, 1)


def block_scores(query_block, key_heads, bias_vec, row_start, length, causal):
    raw_scores = (
        jnp.einsum("qcgd,kcd->cgqk", query_block, key_heads, preferred_element_type=jnp.float32)
        * score_scale
    )
    rows_here = row_start + jnp.arange(query_block.shape[0], dtype=jnp.int32)
    columns = jnp.arange(key_heads.shape[0], dtype=jnp.int32)
    offset = rows_here[:, None] - columns[None, :]
    allowed = columns[None, :] < length
    if causal:
        bias_block = toeplitz_bias(bias_vec, row_start, query_block.shape[0])
        raw_scores = raw_scores + bias_block.reshape(raw_scores.shape)
        allowed = allowed & (offset >= 0)
    return jnp.where(allowed, raw_scores, masked_fill)


def attend_forward(packed, bias_vec, block_rows, causal):
    queries, key_heads, value_heads, length = packed
    seq_len = queries.shape[0]

    def one_block(block_index):
        row_start = block_index * block_rows
        query_block = lax.dynamic_slice_in_dim(queries, row_start, block_rows, 0)
        scores = block_scores(query_block, key_heads, bias_vec, row_start, length, causal)
        row_max = jnp.max(scores, axis=-1, keepdims=True)
        total_sum = jnp.sum(jnp.exp(scores - row_max), axis=-1, keepdims=True)
        log_total = row_max + jnp.log(total_sum)
        attn_probs = jnp.exp(scores - log_total).astype(jnp.bfloat16)
        context = jnp.einsum(
            "cgqk,kcd->qcgd", attn_probs, value_heads, preferred_element_type=jnp.float32
        )
        return (context.astype(jnp.bfloat16), log_total[..., 0])

    contexts, log_totals = lax.map(one_block, jnp.arange(seq_len // block_rows, dtype=jnp.int32))
    return (contexts.reshape(seq_len, -1), log_totals)


def attend_backward(packed, bias_vec, block_rows, causal):
    queries, key_heads, value_heads, length, log_totals, grad_context = packed
    seq_len = queries.shape[0]
    key_len = key_heads.shape[0]
    heads_local = queries.shape[1] * queries.shape[2]

    def one_block(carry, block_index):
        grad_keys, grad_values, grad_bias = carry
        row_start = block_index * block_rows
        query_block = lax.dynamic_slice_in_dim(queries, row_start, block_rows, 0)
        grad_block = lax.dynamic_slice_in_dim(grad_context, row_start, block_rows, 0)
        scores = block_scores(query_block, key_heads, bias_vec, row_start, length, causal)
        attn_probs = jnp.exp(scores - log_totals[block_index][..., None])
        grad_probs = jnp.einsum(
            "qcgd,kcd->cgqk", grad_block, value_heads, preferred_element_type=jnp.float32
        )
        row_delta = jnp.sum(attn_probs * grad_probs, axis=-1, keepdims=True)
        grad_scores = (attn_probs * (grad_probs - row_delta)).astype(jnp.bfloat16)
        grad_query = (
            jnp.einsum("cgqk,kcd->qcgd", grad_scores, key_heads, preferred_element_type=jnp.float32)
            * score_scale
        )
        grad_keys = (
            grad_keys
            + jnp.einsum(
                "cgqk,qcgd->kcd", grad_scores, query_block, preferred_element_type=jnp.float32
            )
            * score_scale
        )
        grad_values = grad_values + jnp.einsum(
            "cgqk,qcgd->kcd",
            attn_probs.astype(jnp.bfloat16),
            grad_block,
            preferred_element_type=jnp.float32,
        )
        if causal:
            flat_grads = grad_scores.astype(jnp.float32).reshape(heads_local, block_rows, key_len)
            grad_bias = grad_bias + diagonal_sums(flat_grads, row_start)
        return ((grad_keys, grad_values, grad_bias), grad_query.astype(jnp.bfloat16))

    zeros_heads = jnp.zeros(key_heads.shape, jnp.float32)
    initial = (zeros_heads, zeros_heads, jnp.zeros((heads_local, key_len), jnp.float32))
    finals, grad_queries = lax.scan(
        one_block, initial, jnp.arange(seq_len // block_rows, dtype=jnp.int32)
    )
    grad_keys, grad_values, grad_bias = finals
    return (
        grad_queries.reshape(seq_len, -1),
        grad_keys.astype(jnp.bfloat16),
        grad_values.astype(jnp.bfloat16),
        grad_bias,
    )


def adam_update(weight, gradient, first_moment, second_moment, factor, decay_now, rate):
    clipped = gradient * factor
    first_new = beta_one * first_moment + (1.0 - beta_one) * clipped
    second_new = beta_two * second_moment + (1.0 - beta_two) * clipped * clipped
    first_hat = first_new / (1.0 - beta_one**STEP)
    second_hat = second_new / (1.0 - beta_two**STEP)
    weight_new = weight - rate * (
        first_hat / (jnp.sqrt(second_hat) + adam_epsilon) + decay_now * weight
    )
    return (first_new, second_new, weight_new)


def per_device(
    rows_in,
    memory,
    lengths,
    mem_lengths,
    cotangent,
    query_w,
    keyval_w,
    out_w,
    cross_query_w,
    cross_keyval_w,
    cross_out_w,
    gateup_w,
    down_w,
    gains,
    rel_table,
    query_m,
    keyval_m,
    out_m,
    cross_query_m,
    cross_keyval_m,
    cross_out_m,
    gateup_m,
    down_m,
    gains_m,
    rel_table_m,
    query_v,
    keyval_v,
    out_v,
    cross_query_v,
    cross_keyval_v,
    cross_out_v,
    gateup_v,
    down_v,
    gains_v,
    rel_table_v,
):
    (
        w_query,
        w_keyval,
        w_out,
        w_cross_query,
        w_cross_keyval,
        w_cross_out,
        w_gateup,
        w_down,
        gain_low,
        table_low,
    ) = (
        lax.all_gather(query_w.astype(jnp.bfloat16), "dp", axis=0, tiled=True),
        lax.all_gather(keyval_w.astype(jnp.bfloat16), "dp", axis=1, tiled=True),
        lax.all_gather(out_w.astype(jnp.bfloat16), "dp", axis=1, tiled=True),
        lax.all_gather(cross_query_w.astype(jnp.bfloat16), "dp", axis=0, tiled=True),
        lax.all_gather(cross_keyval_w.astype(jnp.bfloat16), "dp", axis=1, tiled=True),
        lax.all_gather(cross_out_w.astype(jnp.bfloat16), "dp", axis=1, tiled=True),
        lax.all_gather(gateup_w.astype(jnp.bfloat16), "dp", axis=1, tiled=True),
        lax.all_gather(down_w.astype(jnp.bfloat16), "dp", axis=1, tiled=True),
        lax.all_gather(gains.astype(jnp.bfloat16), "dp", axis=1, tiled=True),
        lax.all_gather(rel_table.astype(jnp.bfloat16), "dp", axis=1, tiled=True),
    )
    kv_local = w_keyval.shape[2] // DH
    heads_local = w_query.shape[1] // DH
    groups = heads_local // kv_local
    block_rows = min(512, SEQ_LEN)
    rows_local = rows_in.shape[0]
    mem_local = memory.shape[0]
    own_start = lax.axis_index("tp") * rows_local
    gain_one = gain_low[0].astype(jnp.float32)
    gain_cross = gain_low[1].astype(jnp.float32)
    gain_three = gain_low[2].astype(jnp.float32)
    onehot = bucket_onehot(SEQ_LEN, table_low.shape[1])
    bias_vec = jnp.dot(table_low.astype(jnp.float32), onehot.T, precision=lax.Precision.HIGHEST)
    rows_group, memory_group = (
        lax.all_gather(rows_in, "tp", axis=0, tiled=True),
        lax.all_gather(memory, "tp", axis=0, tiled=True),
    )
    total_rows = rows_group.shape[0]
    total_memory = memory_group.shape[0]
    seqs_here = total_rows // SEQ_LEN
    residual = rows_in.astype(jnp.float32)
    residual_group = rows_group.astype(jnp.float32)
    normed = rms_scale(residual_group, gain_one).astype(jnp.bfloat16)
    queries = jnp.dot(normed, w_query, preferred_element_type=jnp.float32).astype(jnp.bfloat16)
    keyval = jnp.einsum("ld,cde->cle", normed, w_keyval, preferred_element_type=jnp.float32).astype(
        jnp.bfloat16
    )
    query_seq = queries.reshape(seqs_here, SEQ_LEN, kv_local, groups, DH)
    key_seq = keyval[0].reshape(seqs_here, SEQ_LEN, kv_local, DH)
    value_seq = keyval[1].reshape(seqs_here, SEQ_LEN, kv_local, DH)
    contexts, log_totals = lax.map(
        lambda packed: attend_forward(packed, bias_vec, block_rows, True),
        (query_seq, key_seq, value_seq, lengths),
    )
    context = contexts.reshape(total_rows, heads_local * DH)
    self_branch = lax.psum_scatter(
        jnp.dot(context, w_out, preferred_element_type=jnp.float32),
        "tp",
        scatter_dimension=0,
        tiled=True,
    )
    middle_own = residual + self_branch
    middle_group = lax.all_gather(middle_own, "tp", axis=0, tiled=True)
    normed_cross = rms_scale(middle_group, gain_cross).astype(jnp.bfloat16)
    cross_queries = jnp.dot(normed_cross, w_cross_query, preferred_element_type=jnp.float32).astype(
        jnp.bfloat16
    )
    memory_kv = jnp.einsum(
        "md,cde->cme", memory_group, w_cross_keyval, preferred_element_type=jnp.float32
    ).astype(jnp.bfloat16)
    cross_query_seq = cross_queries.reshape(seqs_here, SEQ_LEN, kv_local, groups, DH)
    memory_key_seq = memory_kv[0].reshape(seqs_here, MEM, kv_local, DH)
    memory_value_seq = memory_kv[1].reshape(seqs_here, MEM, kv_local, DH)
    cross_contexts, cross_logs = lax.map(
        lambda packed: attend_forward(packed, None, block_rows, False),
        (cross_query_seq, memory_key_seq, memory_value_seq, mem_lengths),
    )
    cross_context = cross_contexts.reshape(total_rows, heads_local * DH)
    cross_branch = lax.psum_scatter(
        jnp.dot(cross_context, w_cross_out, preferred_element_type=jnp.float32),
        "tp",
        scatter_dimension=0,
        tiled=True,
    )
    middle_two = middle_own + cross_branch
    normed_three = rms_scale(middle_two, gain_three).astype(jnp.bfloat16)
    hidden_in, grad_out_rows = (
        lax.all_gather(normed_three, "tp", axis=0, tiled=True),
        lax.all_gather(cotangent, "tp", axis=0, tiled=True),
    )
    gate_up = jnp.einsum("ld,cdf->clf", hidden_in, w_gateup, preferred_element_type=jnp.float32)
    hidden = gelu_pair(gate_up[0], gate_up[1]).astype(jnp.bfloat16)
    hidden_out = lax.psum_scatter(
        jnp.dot(hidden, w_down, preferred_element_type=jnp.float32).astype(jnp.bfloat16),
        "tp",
        scatter_dimension=0,
        tiled=True,
    ).astype(jnp.float32)
    block_out = (middle_two + hidden_out).astype(jnp.bfloat16)
    grad_hidden = jnp.einsum("ld,fd->lf", grad_out_rows, w_down, preferred_element_type=jnp.float32)
    grad_down = jnp.einsum("lf,ld->fd", hidden, grad_out_rows, preferred_element_type=jnp.float32)
    unused, pull_gelu = jax.vjp(gelu_pair, gate_up[0], gate_up[1])
    grad_gate, grad_upper = pull_gelu(grad_hidden)
    grad_pair = jnp.stack([grad_gate, grad_upper]).astype(jnp.bfloat16)
    grad_gateup = jnp.einsum(
        "ld,clf->cdf", hidden_in, grad_pair, preferred_element_type=jnp.float32
    )
    grad_normed_three = lax.psum_scatter(
        jnp.einsum("clf,cdf->ld", grad_pair, w_gateup, preferred_element_type=jnp.float32),
        "tp",
        scatter_dimension=0,
        tiled=True,
    )
    unused_three, pull_three = jax.vjp(rms_scale, middle_two, gain_three)
    grad_mid_two_norm, grad_gain_three = pull_three(grad_normed_three)
    grad_middle_two = cotangent.astype(jnp.float32) + grad_mid_two_norm
    grad_middle_two_group = lax.all_gather(grad_middle_two, "tp", axis=0, tiled=True)
    grad_cross_branch = grad_middle_two_group.astype(jnp.bfloat16)
    grad_cross_out_w = jnp.einsum(
        "lh,ld->hd", cross_context, grad_cross_branch, preferred_element_type=jnp.float32
    )
    grad_cross_context = jnp.einsum(
        "ld,hd->lh", grad_cross_branch, w_cross_out, preferred_element_type=jnp.float32
    ).astype(jnp.bfloat16)
    grad_cross_context_seq = grad_cross_context.reshape(seqs_here, SEQ_LEN, kv_local, groups, DH)
    grad_cq_seq, grad_mk_seq, grad_mv_seq, unused_bias = lax.map(
        lambda packed: attend_backward(packed, None, block_rows, False),
        (
            cross_query_seq,
            memory_key_seq,
            memory_value_seq,
            mem_lengths,
            cross_logs,
            grad_cross_context_seq,
        ),
    )
    grad_cross_queries = grad_cq_seq.reshape(total_rows, heads_local * DH)
    grad_memory_kv = jnp.stack(
        [
            grad_mk_seq.reshape(total_memory, kv_local * DH),
            grad_mv_seq.reshape(total_memory, kv_local * DH),
        ]
    )
    grad_cross_query_w = jnp.einsum(
        "ld,lh->dh", normed_cross, grad_cross_queries, preferred_element_type=jnp.float32
    )
    grad_cross_keyval_w = jnp.einsum(
        "md,cme->cde", memory_group, grad_memory_kv, preferred_element_type=jnp.float32
    )
    grad_normed_cross = lax.psum(
        jnp.einsum(
            "lh,dh->ld", grad_cross_queries, w_cross_query, preferred_element_type=jnp.float32
        ),
        "tp",
    )
    unused_cross, pull_cross = jax.vjp(lambda rows: rms_scale(rows, gain_cross), middle_group)
    (grad_mid_norm_group,) = pull_cross(grad_normed_cross)
    grad_gain_cross = gain_term(
        lax.dynamic_slice_in_dim(grad_normed_cross, own_start, rows_local, 0), middle_own
    )
    grad_middle_group = grad_middle_two_group + grad_mid_norm_group
    grad_branch = grad_middle_group.astype(jnp.bfloat16)
    grad_out_w = jnp.einsum("lh,ld->hd", context, grad_branch, preferred_element_type=jnp.float32)
    grad_context = jnp.einsum(
        "ld,hd->lh", grad_branch, w_out, preferred_element_type=jnp.float32
    ).astype(jnp.bfloat16)
    grad_context_seq = grad_context.reshape(seqs_here, SEQ_LEN, kv_local, groups, DH)
    grad_q_seq, grad_k_seq, grad_v_seq, grad_bias_seq = lax.map(
        lambda packed: attend_backward(packed, bias_vec, block_rows, True),
        (query_seq, key_seq, value_seq, lengths, log_totals, grad_context_seq),
    )
    grad_queries = grad_q_seq.reshape(total_rows, heads_local * DH)
    grad_keyvals = jnp.stack(
        [
            grad_k_seq.reshape(total_rows, kv_local * DH),
            grad_v_seq.reshape(total_rows, kv_local * DH),
        ]
    )
    grad_table = jnp.dot(jnp.sum(grad_bias_seq, axis=0), onehot, precision=lax.Precision.HIGHEST)
    grad_query_w = jnp.einsum("ld,lh->dh", normed, grad_queries, preferred_element_type=jnp.float32)
    grad_keyval_w = jnp.einsum(
        "ld,cle->cde", normed, grad_keyvals, preferred_element_type=jnp.float32
    )
    row_total = rows_local + mem_local
    count_dev = row_total * lax.axis_size("tp") // row_total
    from_rows = jnp.einsum("lh,dh->ld", grad_queries, w_query, preferred_element_type=jnp.float32)
    from_rows = from_rows + jnp.einsum(
        "cle,cde->ld", grad_keyvals, w_keyval, preferred_element_type=jnp.float32
    )
    from_memory = jnp.einsum(
        "cme,cde->md", grad_memory_kv, w_cross_keyval, preferred_element_type=jnp.float32
    )
    joined = jnp.concatenate(
        [
            from_rows.reshape(count_dev, rows_local, -1),
            from_memory.reshape(count_dev, mem_local, -1),
        ],
        axis=1,
    )
    combined = lax.psum_scatter(
        joined.reshape(count_dev * row_total, -1).astype(jnp.bfloat16),
        "tp",
        scatter_dimension=0,
        tiled=True,
    ).astype(jnp.float32)
    grad_normed = combined[:rows_local]
    grad_memory = combined[rows_local:]
    unused_one, pull_one = jax.vjp(rms_scale, residual, gain_one)
    grad_res_norm, grad_gain_one = pull_one(grad_normed)
    grad_rows = (
        lax.dynamic_slice_in_dim(grad_middle_group, own_start, rows_local, 0) + grad_res_norm
    )
    reduced = (
        lax.psum_scatter(grad_query_w, "dp", scatter_dimension=0, tiled=True),
        lax.psum_scatter(grad_keyval_w, "dp", scatter_dimension=1, tiled=True),
        lax.psum_scatter(grad_out_w, "dp", scatter_dimension=1, tiled=True),
        lax.psum_scatter(grad_cross_query_w, "dp", scatter_dimension=0, tiled=True),
        lax.psum_scatter(grad_cross_keyval_w, "dp", scatter_dimension=1, tiled=True),
        lax.psum_scatter(grad_cross_out_w, "dp", scatter_dimension=1, tiled=True),
        lax.psum_scatter(grad_gateup, "dp", scatter_dimension=1, tiled=True),
        lax.psum_scatter(grad_down, "dp", scatter_dimension=1, tiled=True),
        lax.psum_scatter(grad_table, "dp", scatter_dimension=1, tiled=True),
    )
    squares = jnp.zeros((), jnp.float32)
    for piece in reduced:
        squares = squares + jnp.sum(piece * piece)
    gain_terms = jnp.stack([grad_gain_one, grad_gain_cross, grad_gain_three])
    squares_all, gains_full = lax.psum((squares, gain_terms), ("dp", "tp"))
    grad_norm = jnp.sqrt(squares_all + jnp.sum(gains_full * gains_full))
    factor = clip_limit / jnp.maximum(grad_norm, clip_limit)
    gains_grad = lax.dynamic_slice_in_dim(
        gains_full, lax.axis_index("dp") * gains.shape[1], gains.shape[1], 1
    )
    grad_list = (
        reduced[0],
        reduced[1],
        reduced[2],
        reduced[3],
        reduced[4],
        reduced[5],
        reduced[6],
        reduced[7],
        gains_grad,
        reduced[8],
    )
    params = (
        query_w,
        keyval_w,
        out_w,
        cross_query_w,
        cross_keyval_w,
        cross_out_w,
        gateup_w,
        down_w,
        gains,
        rel_table,
    )
    firsts = (
        query_m,
        keyval_m,
        out_m,
        cross_query_m,
        cross_keyval_m,
        cross_out_m,
        gateup_m,
        down_m,
        gains_m,
        rel_table_m,
    )
    seconds = (
        query_v,
        keyval_v,
        out_v,
        cross_query_v,
        cross_keyval_v,
        cross_out_v,
        gateup_v,
        down_v,
        gains_v,
        rel_table_v,
    )
    rates = update_rates()
    new_firsts = []
    new_seconds = []
    new_weights = []
    for position in range(10):
        decay_now = decay_rate if position < 8 else 0.0
        first_new, second_new, weight_new = adam_update(
            params[position],
            grad_list[position],
            firsts[position],
            seconds[position],
            factor,
            decay_now,
            rates[position],
        )
        new_firsts.append(first_new)
        new_seconds.append(second_new)
        new_weights.append(weight_new)
    return (
        block_out,
        grad_rows,
        grad_memory,
        grad_norm,
        new_firsts[0],
        new_firsts[1],
        new_firsts[2],
        new_firsts[3],
        new_firsts[4],
        new_firsts[5],
        new_firsts[6],
        new_firsts[7],
        new_firsts[8],
        new_firsts[9],
        new_seconds[0],
        new_seconds[1],
        new_seconds[2],
        new_seconds[3],
        new_seconds[4],
        new_seconds[5],
        new_seconds[6],
        new_seconds[7],
        new_seconds[8],
        new_seconds[9],
        new_weights[0],
        new_weights[1],
        new_weights[2],
        new_weights[3],
        new_weights[4],
        new_weights[5],
        new_weights[6],
        new_weights[7],
        new_weights[8],
        new_weights[9],
    )


def solution(mesh):
    return jax.shard_map(
        per_device,
        mesh=mesh,
        in_specs=(
            P(("dp", "tp"), None),
            P(("dp", "tp"), None),
            P("dp"),
            P("dp"),
            P(("dp", "tp"), None),
            P("dp", "tp"),
            P(None, "dp", "tp"),
            P("tp", "dp"),
            P("dp", "tp"),
            P(None, "dp", "tp"),
            P("tp", "dp"),
            P(None, "dp", "tp"),
            P("tp", "dp"),
            P(None, "dp"),
            P("tp", "dp"),
            P("dp", "tp"),
            P(None, "dp", "tp"),
            P("tp", "dp"),
            P("dp", "tp"),
            P(None, "dp", "tp"),
            P("tp", "dp"),
            P(None, "dp", "tp"),
            P("tp", "dp"),
            P(None, "dp"),
            P("tp", "dp"),
            P("dp", "tp"),
            P(None, "dp", "tp"),
            P("tp", "dp"),
            P("dp", "tp"),
            P(None, "dp", "tp"),
            P("tp", "dp"),
            P(None, "dp", "tp"),
            P("tp", "dp"),
            P(None, "dp"),
            P("tp", "dp"),
        ),
        out_specs=(
            P(("dp", "tp"), None),
            P(("dp", "tp"), None),
            P(("dp", "tp"), None),
            P(),
            P("dp", "tp"),
            P(None, "dp", "tp"),
            P("tp", "dp"),
            P("dp", "tp"),
            P(None, "dp", "tp"),
            P("tp", "dp"),
            P(None, "dp", "tp"),
            P("tp", "dp"),
            P(None, "dp"),
            P("tp", "dp"),
            P("dp", "tp"),
            P(None, "dp", "tp"),
            P("tp", "dp"),
            P("dp", "tp"),
            P(None, "dp", "tp"),
            P("tp", "dp"),
            P(None, "dp", "tp"),
            P("tp", "dp"),
            P(None, "dp"),
            P("tp", "dp"),
            P("dp", "tp"),
            P(None, "dp", "tp"),
            P("tp", "dp"),
            P("dp", "tp"),
            P(None, "dp", "tp"),
            P("tp", "dp"),
            P(None, "dp", "tp"),
            P("tp", "dp"),
            P(None, "dp"),
            P("tp", "dp"),
        ),
        check_vma=False,
    )
```

profile of v0, /device:TPU:0, one launch (start us, length us, event | category | flops | bytes accessed | tf_op | source)
XLA Modules:
  0.0 2104.5 jit_solution(1245043347081716344)
XLA Ops:
  69.0 333.0 %while.102 = (s32[]{:T(128)}, bf16[2,512,2,2,64]{1,4,3,2,0:T(8,128)(2,1)S(1)}, f32[2,2,2,512]{3,2,1,0:T(2,128)S(1)}, s32[]{:T(128)}, s32[2]{0:T(128)S(1)}, /*ind...) while((s32[]{:T(128)}, ...), condition=%wide.region_5.6_spmd, body=%wide.region_2.5_spmd.sunk | while | flops 555363840 | bytes 182720720 | solution.py:137
  164.6 67.7 %rev.24 = f32[4,512,1024]{2,1,0:T(8,128)} reverse(f32[4,512,1024]{2,1,0:T(8,128)} %slice.156), dimensions={2} | reverse | bytes 16777216 | tf_op jit(solution)/shard_map/while/body/eval_jaxpr/while/body/eval_jaxpr/jit(_flip)/rev | solution.py:87
  318.2 67.7 %rev.24 = f32[4,512,1024]{2,1,0:T(8,128)} reverse(f32[4,512,1024]{2,1,0:T(8,128)} %slice.156), dimensions={2} | reverse | bytes 16777216 | tf_op jit(solution)/shard_map/while/body/eval_jaxpr/while/body/eval_jaxpr/jit(_flip)/rev | solution.py:87
  406.2 76.4 %reduce-scatter.15.cloned.1.call-done = f32[256,1024]{1,0:T(8,128)} async-done(((f32[1024,1024]{1,0:T(8,128)}), f32[256,1024]{1,0:T(8,128)}) %reduce-scatter.15.cloned.1.call-update) | async-done | bytes 1048592 | tf_op jit(solution)/shard_map/reduce_scatter | solution.py:301
  517.2 78.0 %all-gather.12.cloned.1.call-done = f32[1024,1024]{1,0:T(8,128)} async-done(((f32[256,1024]{1,0:T(8,128)}), f32[1024,1024]{1,0:T(8,128)}) %all-gather.12.cloned.1.call-update) | async-done | bytes 4194320 | tf_op jit(solution)/shard_map/all_gather | solution.py:308
  614.7 73.4 %reduce-scatter.17.cloned.1.call-done = f32[256,1024]{1,0:T(8,128)} async-done(((f32[1024,1024]{1,0:T(8,128)}), f32[256,1024]{1,0:T(8,128)}) %reduce-scatter.17.cloned.1.call-update) | async-done | bytes 1048592 | tf_op jit(solution)/shard_map/reduce_scatter | solution.py:324
  693.3 43.4 %all-gather.16.cloned.1.call-done = bf16[1024,1024]{1,0:T(8,128)(2,1)} async-done(((bf16[256,1024]{1,0:T(8,128)(2,1)}), bf16[1024,1024]{1,0:T(8,128)(2,1)}) %all-gather.16.cloned.1.call-update) | async-done | bytes 2097168 | tf_op jit(solution)/shard_map/all_gather | solution.py:333
  763.0 47.2 %all-gather.22.cloned.1.call-done = bf16[1024,1024]{1,0:T(8,128)(2,1)} async-done(((bf16[256,1024]{1,0:T(8,128)(2,1)}), bf16[1024,1024]{1,0:T(8,128)(2,1)}) %all-gather.22.cloned.1.call-update) | async-done | bytes 2097168 | tf_op jit(solution)/shard_map/all_gather | solution.py:334
  830.5 70.6 %reduce-scatter.21.cloned.1.call-done = f32[256,1024]{1,0:T(8,128)} async-done(((f32[1024,1024]{1,0:T(8,128)}), f32[256,1024]{1,0:T(8,128)}) %reduce-scatter.21.cloned.1.call-update) | async-done | bytes 1048592 | tf_op jit(solution)/shard_map/reduce_scatter | solution.py:353
  903.2 44.3 %reduce-scatter.19.cloned.1.call-done = bf16[256,1024]{1,0:T(8,128)(2,1)} async-done(((bf16[1024,1024]{1,0:T(8,128)(2,1)}), bf16[256,1024]{1,0:T(8,128)(2,1)}) %reduce-scatter.19.cloned.1.call-update) | async-done | bytes 524304 | tf_op jit(solution)/shard_map/reduce_scatter | solution.py:338
  950.9 79.4 %all-gather.24.cloned.1.call-done = f32[1024,1024]{1,0:T(8,128)} async-done(((f32[256,1024]{1,0:T(8,128)}), f32[1024,1024]{1,0:T(8,128)}) %all-gather.24.cloned.1.call-update) | async-done | bytes 4194320 | tf_op jit(solution)/shard_map/all_gather | solution.py:362
  1033.3 19.8 while.104
  1081.7 128.6 %all-reduce.6.cloned.1.call-done = f32[1024,1024]{1,0:T(8,128)} async-done(((f32[1024,1024]{1,0:T(8,128)}), f32[1024,1024]{1,0:T(8,128)}) %all-reduce.6.cloned.1.call-update) | async-done | bytes 4194320 | tf_op jit(solution)/shard_map/psum | solution.py:395
  1223.0 622.8 %while.105 = (s32[]{:T(128)}, f32[1024,2,64]{0,2,1:T(8,128)S(1)}, f32[1024,2,64]{0,2,1:T(8,128)S(1)}, f32[4,1024]{1,0:T(4,128)S(1)}, bf16[2,512,2,2,64]{1,4,3,2,...) while((s32[]{:T(128)}, f32[1024,2,64]{0,2,1:T(8,128)S(1)}, ...), condition=%wide.region_25.26_spmd.clone, body=%wide.region_22.25_spmd.clone.sunk | while | flops 1370893824 | bytes 418650624 | solution.py:183
  1307.5 67.7 %rev.25 = f32[4,512,1024]{2,1,0:T(8,128)} reverse(f32[4,512,1024]{2,1,0:T(8,128)} %slice.159), dimensions={2} | reverse | bytes 16777216 | tf_op jit(solution)/shard_map/while/body/eval_jaxpr/while/body/eval_jaxpr/jit(_flip)/rev | solution.py:87
  1393.0 67.8 %rev.26 = f32[4,512,1024]{2,1,0:T(8,128)} reverse(f32[4,512,1024]{2,1,0:T(8,128)} %bitcast_convert_fusion.3), dimensions={2} | reverse | bytes 16777216 | tf_op jit(solution)/shard_map/while/body/eval_jaxpr/while/body/eval_jaxpr/jit(_flip)/rev | solution.py:92
  1465.9 19.9 copy.282
  1614.5 67.7 %rev.25 = f32[4,512,1024]{2,1,0:T(8,128)} reverse(f32[4,512,1024]{2,1,0:T(8,128)} %slice.159), dimensions={2} | reverse | bytes 16777216 | tf_op jit(solution)/shard_map/while/body/eval_jaxpr/while/body/eval_jaxpr/jit(_flip)/rev | solution.py:87
  1700.0 67.8 %rev.26 = f32[4,512,1024]{2,1,0:T(8,128)} reverse(f32[4,512,1024]{2,1,0:T(8,128)} %bitcast_convert_fusion.3), dimensions={2} | reverse | bytes 16777216 | tf_op jit(solution)/shard_map/while/body/eval_jaxpr/while/body/eval_jaxpr/jit(_flip)/rev | solution.py:92
  1773.0 19.9 copy.282
  1893.6 31.9 %reduce-scatter.27.cloned.1.call-done = f32[2,128,128]{1,2,0:T(8,128)} async-done(((f32[2,1024,128]{1,2,0:T(8,128)}), f32[2,128,128]{1,2,0:T(8,128)}) %reduce-scatter.27.cloned.1.call-update) | async-done | bytes 131088 | tf_op jit(solution)/shard_map/reduce_scatter | solution.py:460
  1928.4 36.7 %reduce-scatter.29.cloned.1.call-done = f32[256,128]{1,0:T(8,128)} async-done(((f32[256,1024]{1,0:T(8,128)}), f32[256,128]{1,0:T(8,128)}) %reduce-scatter.29.cloned.1.call-update) | async-done | bytes 131088 | tf_op jit(solution)/shard_map/reduce_scatter | solution.py:461
  1971.1 56.6 %reduce-scatter.23.cloned.1.call-done = bf16[384,1024]{1,0:T(8,128)(2,1)} async-done(((bf16[1536,1024]{1,0:T(8,128)(2,1)}), bf16[384,1024]{1,0:T(8,128)(2,1)}) %reduce-scatter.23.cloned.1.call-update) | async-done | bytes 786448 | tf_op jit(solution)/shard_map/reduce_scatter | solution.py:445
  2032.2 40.5 %all-reduce.3 = (f32[]{:T(128)}, f32[3,1024]{1,0:T(4,128)S(1)}) all-reduce(f32[]{:T(128)S(6)} %add.505, f32[3,1024]{1,0:T(4,128)S(1)} %pad_maximum_fusion.10), channel_id=1, replica_groups=mesh['dp'=8,'tp'=4] {'dp','tp'}, use_global_device_ids=true, to_apply=%region_47.48 | all-reduce | flops 3073 | bytes 24584 | tf_op jit(solution)/shard_map/psum | solution.py:473
  (518 shorter events, 786.5 us)
Async XLA Ops:
  8.0 55.0 %all-gather.10.cloned.1.call-start = ((), (), s32[]{:S(2)}) async-start(), calls=%async_computation.13 | async-start | bytes 2621440 | tf_op jit(solution)/shard_map/all_gather | solution.py:280
  8.8 473.9 %reduce-scatter.15.cloned.1.call-start = ((), (), s32[]{:S(2)}) async-start(), calls=%async_computation.14 | async-start | bytes 5242880 | tf_op jit(solution)/shard_map/reduce_scatter | solution.py:301
  405.4 109.8 %all-gather.14.cloned.1.call-start = ((), (), s32[]{:S(2)}) async-start(), calls=%async_computation.16 | async-start | bytes 1310720 | tf_op jit(solution)/shard_map/all_gather | solution.py:281
  406.1 189.0 %all-gather.12.cloned.1.call-start = ((), (), s32[]{:S(2)}) async-start(), calls=%async_computation.15 | async-start | bytes 5242880 | tf_op jit(solution)/shard_map/all_gather | solution.py:308
  485.6 202.6 %reduce-scatter.17.cloned.1.call-start = ((), (), s32[]{:S(2)}) async-start(), calls=%async_computation.17 | async-start | bytes 5242880 | tf_op jit(solution)/shard_map/reduce_scatter | solution.py:324
  612.7 80.7 %all-gather.18.cloned.1.call-start = ((), (), s32[]{:S(2)}) async-start(), calls=%async_computation.19 | async-start | bytes 3244032 | tf_op jit(solution)/shard_map/all_gather | solution.py:262
  614.7 122.1 %all-gather.16.cloned.1.call-start = ((), (), s32[]{:S(2)}) async-start(), calls=%async_computation.18 | async-start | bytes 2621440 | tf_op jit(solution)/shard_map/all_gather | solution.py:333
  690.6 72.4 %all-gather.20.cloned.1.call-start = ((), (), s32[]{:S(2)}) async-start(), calls=%async_computation.20 | async-start | bytes 1622016 | tf_op jit(solution)/shard_map/all_gather | solution.py:263
  692.3 117.9 %all-gather.22.cloned.1.call-start = ((), (), s32[]{:S(2)}) async-start(), calls=%async_computation.22 | async-start | bytes 2621440 | tf_op jit(solution)/shard_map/all_gather | solution.py:334
  693.0 208.0 %reduce-scatter.21.cloned.1.call-start = ((), (), s32[]{:S(2)}) async-start(), calls=%async_computation.23 | async-start | bytes 5242880 | tf_op jit(solution)/shard_map/reduce_scatter | solution.py:353
  825.4 122.0 %reduce-scatter.19.cloned.1.call-start = ((), (), s32[]{:S(2)}) async-start(), calls=%async_computation.21 | async-start | bytes 2621440 | tf_op jit(solution)/shard_map/reduce_scatter | solution.py:338
  830.5 199.8 %all-gather.24.cloned.1.call-start = ((), (), s32[]{:S(2)}) async-start(), calls=%async_computation.24 | async-start | bytes 5242880 | tf_op jit(solution)/shard_map/all_gather | solution.py:362
  950.4 259.9 %all-reduce.6.cloned.1.call-start = ((), (), s32[]{:S(2)}) async-start(), calls=%async_computation.25 | async-start | bytes 8388608 | tf_op jit(solution)/shard_map/psum | solution.py:395
  1056.6 811.0 %reduce-scatter.39.cloned.1.call-start = ((), (), s32[]{:S(2)}) async-start(), calls=%async_computation.34 | async-start | bytes 3244032 | tf_op jit(solution)/shard_map/reduce_scatter | solution.py:466
  1062.0 807.4 %reduce-scatter.37.cloned.1.call-start = ((), (), s32[]{:S(2)}) async-start(), calls=%async_computation.33 | async-start | bytes 6488064 | tf_op jit(solution)/shard_map/reduce_scatter | solution.py:465
  1070.1 801.2 %reduce-scatter.33.cloned.1.call-start = ((), (), s32[]{:S(2)}) async-start(), calls=%async_computation.31 | async-start | bytes 1179648 | tf_op jit(solution)/shard_map/reduce_scatter | solution.py:463
  1073.4 799.4 %reduce-scatter.35.cloned.1.call-start = ((), (), s32[]{:S(2)}) async-start(), calls=%async_computation.32 | async-start | bytes 1179648 | tf_op jit(solution)/shard_map/reduce_scatter | solution.py:464
  1077.5 796.9 %reduce-scatter.31.cloned.1.call-start = ((), (), s32[]{:S(2)}) async-start(), calls=%async_computation.30 | async-start | bytes 1179648 | tf_op jit(solution)/shard_map/reduce_scatter | solution.py:462
  1081.7 810.3 %reduce-scatter.25.cloned.1.call-start = ((), (), s32[]{:S(2)}) async-start(), calls=%async_computation.27 | async-start | bytes 1179648 | tf_op jit(solution)/shard_map/reduce_scatter | solution.py:459
  1222.9 624.4 %copy-start.73 = (f32[1,1024]{1,0:T(1,128)S(1)}, f32[1,1024]{1,0:T(1,128)}, u32[]{:S(2)}) copy-start(f32[1,1024]{1,0:T(1,128)} %copy-done.72) | copy-start | bytes 12292
  1222.9 624.4 %copy-start.82 = (f32[1024]{0:T(1024)S(1)}, f32[1024]{0:T(1024)}, u32[]{:S(2)}) copy-start(f32[1024]{0:T(1024)} %copy-done.81) | copy-start | bytes 12292
  1851.0 74.5 %reduce-scatter.27.cloned.1.call-start = ((), (), s32[]{:S(2)}) async-start(), calls=%async_computation.28 | async-start | bytes 1179648 | tf_op jit(solution)/shard_map/reduce_scatter | solution.py:460
  1855.0 110.0 %reduce-scatter.29.cloned.1.call-start = ((), (), s32[]{:S(2)}) async-start(), calls=%async_computation.29 | async-start | bytes 1179648 | tf_op jit(solution)/shard_map/reduce_scatter | solution.py:461
  1859.1 168.6 %reduce-scatter.23.cloned.1.call-start = ((), (), s32[]{:S(2)}) async-start(), calls=%async_computation.26 | async-start | bytes 3932160 | tf_op jit(solution)/shard_map/reduce_scatter | solution.py:445
  (97 other events, 3768.4 us)
Sparse Core Ops, SparseCore 0:
  10.4 48.6 all-gather.9
  405.5 77.0 reduce-scatter.14
  484.3 28.4 all-gather.13
  514.8 80.2 all-gather.11
  612.8 75.2 reduce-scatter.16
  1056.7 153.4 all-reduce.5
Sparse Core Ops, SparseCore 1:
  615.6 30.0 all-gather.17
  690.6 46.0 all-gather.15
  739.0 23.9 all-gather.19
  764.6 45.5 all-gather.21
  825.5 75.5 reduce-scatter.20
  903.5 43.9 reduce-scatter.18
  950.5 79.8 all-gather.23
  1062.0 43.3 reduce-scatter.38
  1108.7 58.8 reduce-scatter.36
  1171.1 35.9 reduce-scatter.32
  1210.4 35.9 reduce-scatter.34
  1249.9 35.9 reduce-scatter.30
  1851.1 34.9 reduce-scatter.24
  1889.6 35.9 reduce-scatter.26
  1929.0 35.9 reduce-scatter.28
  1967.5 60.2 reduce-scatter.22
where the time goes:
time: 2140 us; the launch traced here: 2100 us
  local copies, waits for them, and re-layouts  867 us (41%)
  waiting for transfers between devices  787 us (37%)
  matrix products  143 us (7%)
  blocking collectives  131 us (6%)
  other arithmetic  100 us (5%)
  loops' own time  48.2 us (2%)
  between operations  26.5 us (1%)
    rev x4, local copies, waits for them, and re-layouts, toeplitz_bias(): return jnp.flip(shifted, axis=2)  271 us
    while x38, local copies, waits for them, and re-layouts  210 us
    rev x2, local copies, waits for them, and re-layouts, diagonal_sums(): flipped = jnp.flip(grads, axis=2)  136 us
    psum x1, waiting for transfers between devices, per_device(): lax.psum(jnp.einsum('lh,dh->ld', grad_cross_queries, w_cross_query, prefe...  129 us
    another operation x8, local copies, waits for them, and re-layouts, toeplitz_bias(): tiled = jnp.tile(strip, (1, block_rows + 1))[:, :block_rows * (width + 1)]  91.2 us
    all_gather x1, waiting for transfers between devices, per_device(): lax.all_gather(grad_middle_two, 'tp', axis=0, tiled=True)  79.4 us
    all_gather x1, waiting for transfers between devices, per_device(): middle_group = lax.all_gather(middle_own, 'tp', axis=0, tiled=True)  78 us
    reduce_scatter x1, waiting for transfers between devices, per_device(): lax.psum_scatter(jnp.dot(context, w_out, preferred_element_type=jnp.float...  76.4 us
  transfers between devices with their start and end apart: 22, of which 13 were waited for; matrix products, arithmetic and copies ran while one was open for 34% of the time, Pallas kernels for 0%

commit v1 on v0

v1 whole, which is shorter than its diff:
```python
import functools
import math

import jax
import jax.numpy as jnp
import numpy as np
from jax import lax
from jax.experimental import pallas as pl
from jax.experimental.pallas import tpu as pltpu
from jax.sharding import PartitionSpec as P

D = 1024
H = 16
DH = 64
FF = 2816
SEQ_LEN = 1024
MEM = 512
STEP = 10

f32 = jnp.float32
bf16 = jnp.bfloat16

bucket_edges = np.array(
    [math.ceil(16.0 * 8.0 ** ((level - 16) / 16.0)) for level in range(17, 32)], dtype=np.int32
)
score_scale = 0.125
masked_fill = -1e30
norm_epsilon = 1e-06
clip_limit = 1.0
beta_one = 0.9
beta_two = 0.95
adam_epsilon = 1e-08
decay_rate = 0.1


def update_rates():
    return (
        D ** (-0.5),
        D ** (-0.5),
        max(1, H * DH * 8 // SEQ_LEN) ** (-0.5),
        D ** (-0.5),
        D ** (-0.5),
        max(1, H * DH * 8 // MEM) ** (-0.5),
        D ** (-0.5),
        FF ** (-0.5),
        1.0,
        0.5,
    )


def dotf(a,b,dims):
    return lax.dot_general(a,b,(dims,((),())),preferred_element_type=f32)

def place(x, src_half, dst_half):
    lane=lax.broadcasted_iota(jnp.int32,x.shape,1)
    y=x if src_half==dst_half else jnp.concatenate([x[:,64:],x[:,:64]],axis=1)
    keep=(lane<64) if dst_half==0 else (lane>=64)
    return jnp.where(keep,y,jnp.zeros_like(y))

def fwd_kernel(causal, groups, scal_ref, q_ref, k_ref, v_ref, *refs):
    if causal: strip_ref, ctx_ref, p_ref = refs
    else: ctx_ref, p_ref = refs
    length=scal_ref[0]; row0=scal_ref[1]
    R=q_ref.shape[0]; K=k_ref.shape[0]
    col=lax.broadcasted_iota(jnp.int32,(R,K),1)
    allowed=col<length
    if causal:
        row=lax.broadcasted_iota(jnp.int32,(R,K),0)+row0
        allowed=allowed&(col<=row)
    k=k_ref[...]; v=v_ref[...]
    heads=2*groups
    outs=[]
    for h in range(heads):
        u=h//groups
        qh=place(q_ref[:,(h//2)*128:(h//2)*128+128]*jnp.bfloat16(0.125),h%2,u)
        s=dotf(qh,k,((1,),(1,)))
        if causal:
            w=strip_ref.shape[-1]
            t=pltpu.roll(jnp.broadcast_to(strip_ref[h:h+1,:] if len(strip_ref.shape)==2 else strip_ref[0,h:h+1,:],(R,w)),0,1,stride=1,stride_axis=0)
            s=s+t[:,:K]
        s=jnp.where(allowed,s,masked_fill)
        m=jnp.max(s,axis=1,keepdims=True)
        e=jnp.exp(s-m)
        p=(e*(1.0/jnp.sum(e,axis=1,keepdims=True))).astype(bf16)
        p_ref[h]=p
        c=dotf(p,v,((1,),(0,))).astype(bf16)
        outs.append(place(c,u,h%2))
    for b in range(heads//2):
        ctx_ref[:,b*128:(b+1)*128]=outs[2*b]+outs[2*b+1]

def attn_fwd(q,k,v,scal,strip,causal):
    R,C=q.shape; K=k.shape[0]
    H=C//DH; KV=k.shape[1]//DH; groups=H//KV; pairs=KV//2
    hp=2*groups
    ins=[pl.BlockSpec(memory_space=pltpu.SMEM),
         pl.BlockSpec((R,hp*DH),lambda p:(0,p)),
         pl.BlockSpec((K,128),lambda p:(0,p)),
         pl.BlockSpec((K,128),lambda p:(0,p))]
    args=[scal,q,k,v]
    if causal:
        ins.append(pl.BlockSpec((1,hp,strip.shape[-1]),lambda p:(p,0,0)))
        args.append(strip.reshape(pairs,hp,-1))
    return pl.pallas_call(functools.partial(fwd_kernel,causal,groups),grid=(pairs,),
        in_specs=ins,
        out_specs=[pl.BlockSpec((R,hp*DH),lambda p:(0,p)),pl.BlockSpec((hp,R,K),lambda p:(p,0,0))],
        out_shape=[jax.ShapeDtypeStruct((R,C),bf16),jax.ShapeDtypeStruct((H,R,K),bf16)],
        compiler_params=pltpu.CompilerParams(vmem_limit_bytes=48<<20),
        name="attend_fwd")(*args)

def bwd_kernel(causal, groups, q_ref, k_ref, v_ref, p_ref, g_ref, *refs):
    if causal: flip_ref, dq_ref, dk_ref, dv_ref, diag_ref = refs
    else: dq_ref, dk_ref, dv_ref = refs
    R=q_ref.shape[0]; K=k_ref.shape[0]
    k=k_ref[...]; v=v_ref[...]
    heads=2*groups
    dqs=[]; dk=None; dv=None
    for h in range(heads):
        u=h//groups; b=(h//2)*128
        qh=place(q_ref[:,b:b+128]*jnp.bfloat16(0.125),h%2,u)
        gh=place(g_ref[:,b:b+128],h%2,u)
        pb=p_ref[h]
        p=pb.astype(f32)
        dp=dotf(gh,v,((1,),(1,)))
        pd=p*dp
        delta=jnp.sum(pd,axis=1,keepdims=True)
        gs=(pd-p*delta).astype(bf16)
        dqs.append(place((dotf(gs,k,((1,),(0,)))*0.125).astype(bf16),u,h%2))
        a=dotf(gs,qh,((0,),(0,)))
        c=dotf(pb,gh,((0,),(0,)))
        dk=a if dk is None else dk+a
        dv=c if dv is None else dv+c
        if causal:
            w=diag_ref.shape[-1]
            fl=dotf(flip_ref[...],gs,((1,),(0,)))
            fl=jnp.concatenate([fl,jnp.zeros((R,w-K),f32)],axis=1)
            diag_ref[0,h:h+1,:]=jnp.sum(pltpu.roll(fl,0,1,stride=1,stride_axis=0),axis=0,keepdims=True)
    for b in range(heads//2):
        dq_ref[:,b*128:(b+1)*128]=dqs[2*b]+dqs[2*b+1]
    dk_ref[...]=dk.astype(bf16); dv_ref[...]=dv.astype(bf16)

def attn_bwd(q,k,v,p,g,causal,W):
    R,C=q.shape; K=k.shape[0]
    H=C//DH; KV=k.shape[1]//DH; groups=H//KV; pairs=KV//2
    hp=2*groups
    ins=[pl.BlockSpec((R,hp*DH),lambda p:(0,p)),
         pl.BlockSpec((K,128),lambda p:(0,p)),
         pl.BlockSpec((K,128),lambda p:(0,p)),
         pl.BlockSpec((hp,R,K),lambda p:(p,0,0)),
         pl.BlockSpec((R,hp*DH),lambda p:(0,p))]
    args=[q,k,v,p,g]
    outs=[pl.BlockSpec((R,hp*DH),lambda p:(0,p)),pl.BlockSpec((K,128),lambda p:(0,p)),pl.BlockSpec((K,128),lambda p:(0,p))]
    shp=[jax.ShapeDtypeStruct((R,C),bf16),jax.ShapeDtypeStruct(k.shape,bf16),jax.ShapeDtypeStruct(k.shape,bf16)]
    if causal:
        ins.append(pl.BlockSpec((R,R),lambda p:(0,0)))
        args.append(jnp.asarray(np.eye(R)[::-1],bf16))
        outs.append(pl.BlockSpec((1,hp,W),lambda p:(p,0,0)))
        shp.append(jax.ShapeDtypeStruct((pairs,hp,W),f32))
    r=pl.pallas_call(functools.partial(bwd_kernel,causal,groups),grid=(pairs,),in_specs=ins,out_specs=outs,out_shape=shp,
        compiler_params=pltpu.CompilerParams(vmem_limit_bytes=48<<20),name="attend_bwd")(*args)
    return r


def bucket_onehot(offsets, buckets):
    offsets = jnp.maximum(offsets, 0)
    passed = jnp.sum((offsets[:, None] >= jnp.asarray(bucket_edges)).astype(jnp.int32), axis=-1)
    index = jnp.where(offsets < 16, offsets, 16 + passed)
    return (index[:, None] == jnp.arange(buckets, dtype=jnp.int32)[None, :]).astype(f32)


def root_of(rows):
    return lax.rsqrt(jnp.mean(rows * rows, axis=-1, keepdims=True) + norm_epsilon)


def norm_rows(rows, gain):
    return (rows * root_of(rows) * gain).astype(bf16)


def norm_back(grad, rows, gain):
    root = root_of(rows)
    scaled = rows * root
    weighted = grad * gain
    grad_rows = root * (weighted - scaled * jnp.mean(weighted * scaled, axis=-1, keepdims=True))
    return grad_rows, jnp.sum(grad * scaled, axis=0)


def ffn_kernel(x_ref, c_ref, wg_ref, wd_ref, out_ref, dx_ref, gg_ref, gd_ref):
    x = x_ref[...]
    c = c_ref[...]
    wg = wg_ref[0, 0]
    wu = wg_ref[0, 1]
    wd = wd_ref[...]
    gate = dotf(x, wg, ((1,), (0,)))
    upper = dotf(x, wu, ((1,), (0,)))
    cubic = math.sqrt(2.0 / math.pi)
    square = gate * gate
    t = jnp.tanh(cubic * gate * (1.0 + 0.044715 * square))
    half = 0.5 * (1.0 + t)
    act = gate * half
    slope = half + 0.5 * gate * (1.0 - t * t) * cubic * (1.0 + 3.0 * 0.044715 * square)
    hidden = (act * upper).astype(bf16)
    grad_hidden = dotf(c, wd, ((1,), (1,)))
    grad_gate = (grad_hidden * upper * slope).astype(bf16)
    grad_upper = (grad_hidden * act).astype(bf16)
    part = dotf(hidden, wd, ((1,), (0,)))
    back = dotf(grad_gate, wg, ((1,), (1,))) + dotf(grad_upper, wu, ((1,), (1,)))
    gd_ref[...] = dotf(hidden, c, ((0,), (0,))).astype(bf16)
    gg_ref[0, 0] = dotf(x, grad_gate, ((0,), (0,))).astype(bf16)
    gg_ref[0, 1] = dotf(x, grad_upper, ((0,), (0,))).astype(bf16)

    @pl.when(pl.program_id(0) == 0)
    def _():
        out_ref[...] = part
        dx_ref[...] = back

    @pl.when(pl.program_id(0) > 0)
    def _():
        out_ref[...] += part
        dx_ref[...] += back


def feed_forward(x, cot, w_gateup, w_down):
    rows, width = x.shape
    blocks, unused, unused_d, units = w_gateup.shape
    whole = pl.BlockSpec((rows, width), lambda i: (0, 0))
    gates = pl.BlockSpec((1, 2, width, units), lambda i: (i, 0, 0, 0))
    downs = pl.BlockSpec((units, width), lambda i: (i, 0))
    return pl.pallas_call(
        ffn_kernel,
        grid=(blocks,),
        in_specs=[whole, whole, gates, downs],
        out_specs=[whole, whole, gates, downs],
        out_shape=[
            jax.ShapeDtypeStruct((rows, width), f32),
            jax.ShapeDtypeStruct((rows, width), f32),
            jax.ShapeDtypeStruct(w_gateup.shape, bf16),
            jax.ShapeDtypeStruct(w_down.shape, bf16),
        ],
        compiler_params=pltpu.CompilerParams(vmem_limit_bytes=56 << 20),
        name="feed_forward",
    )(x, cot, w_gateup, w_down)


def mm(a, b):
    return jnp.dot(a, b, preferred_element_type=f32)


def mm_nt(a, b):
    return dotf(a, b, ((1,), (1,)))


def mm_tn(a, b):
    return dotf(a, b, ((0,), (0,)))


def gather_full(shard, dp_axis, tp_axis):
    part = lax.all_gather(shard, "tp", axis=tp_axis, tiled=True)
    return lax.all_gather(part, "dp", axis=dp_axis, tiled=True)


def scatter_sum(whole, dp_axis, tp_axis):
    part = lax.psum_scatter(whole, "dp", scatter_dimension=dp_axis, tiled=True)
    return lax.psum_scatter(part, "tp", scatter_dimension=tp_axis, tiled=True).astype(f32)


def adam_update(weight, gradient, first_moment, second_moment, factor, decay_now, rate):
    clipped = gradient * factor
    first_new = beta_one * first_moment + (1.0 - beta_one) * clipped
    second_new = beta_two * second_moment + (1.0 - beta_two) * clipped * clipped
    first_hat = first_new / (1.0 - beta_one**STEP)
    second_hat = second_new / (1.0 - beta_two**STEP)
    weight_new = weight - rate * (
        first_hat / (jnp.sqrt(second_hat) + adam_epsilon) + decay_now * weight
    )
    return (first_new, second_new, weight_new)


def per_device(
    rows_in,
    memory,
    lengths,
    mem_lengths,
    cotangent,
    query_w,
    keyval_w,
    out_w,
    cross_query_w,
    cross_keyval_w,
    cross_out_w,
    gateup_w,
    down_w,
    gains,
    rel_table,
    query_m,
    keyval_m,
    out_m,
    cross_query_m,
    cross_keyval_m,
    cross_out_m,
    gateup_m,
    down_m,
    gains_m,
    rel_table_m,
    query_v,
    keyval_v,
    out_v,
    cross_query_v,
    cross_keyval_v,
    cross_out_v,
    gateup_v,
    down_v,
    gains_v,
    rel_table_v,
):
    low = lambda w: w.astype(bf16)
    w_query = gather_full(low(query_w), 0, 1)
    w_keyval = gather_full(low(keyval_w), 1, 2)
    w_out = gather_full(low(out_w), 1, 0)
    w_cross_query = gather_full(low(cross_query_w), 0, 1)
    w_cross_keyval = gather_full(low(cross_keyval_w), 1, 2)
    w_cross_out = gather_full(low(cross_out_w), 1, 0)
    w_gateup = gather_full(low(gateup_w)[None], 2, 0)
    w_down = gather_full(low(down_w), 1, 0)
    gain_low = lax.all_gather(low(gains), "dp", axis=1, tiled=True).astype(f32)
    table_low = gather_full(low(rel_table), 1, 0)
    rows_group = lax.all_gather(rows_in, "tp", axis=0, tiled=True)
    memory_group = lax.all_gather(memory, "tp", axis=0, tiled=True)

    rows_local = rows_in.shape[0]
    key_rows = rows_group.shape[0]
    buckets = table_low.shape[1]
    own_start = lax.axis_index("tp") * rows_local
    width = key_rows + rows_local
    place_index = jnp.arange(width, dtype=jnp.int32)
    signed = jnp.where(place_index >= key_rows, place_index - width, place_index)
    strip = dotf(
        table_low, bucket_onehot(own_start - signed, buckets).astype(bf16), ((1,), (1,))
    )
    diag_onehot = bucket_onehot(own_start + rows_local - 1 - place_index, buckets)

    residual = rows_in.astype(f32)
    normed_group = norm_rows(rows_group.astype(f32), gain_low[0])
    normed = norm_rows(residual, gain_low[0])
    queries = mm(normed, w_query).astype(bf16)
    keys = mm(normed_group, w_keyval[0]).astype(bf16)
    values = mm(normed_group, w_keyval[1]).astype(bf16)
    self_scalars = jnp.stack([lengths[0], own_start.astype(jnp.int32)])
    context, probs = attn_fwd(queries, keys, values, self_scalars, strip, True)
    middle = residual + mm(context, w_out)

    normed_cross = norm_rows(middle, gain_low[1])
    cross_queries = mm(normed_cross, w_cross_query).astype(bf16)
    memory_keys = mm(memory_group, w_cross_keyval[0]).astype(bf16)
    memory_values = mm(memory_group, w_cross_keyval[1]).astype(bf16)
    cross_scalars = jnp.stack([mem_lengths[0], own_start.astype(jnp.int32)])
    cross_context, cross_probs = attn_fwd(
        cross_queries, memory_keys, memory_values, cross_scalars, None, False
    )
    middle_two = middle + mm(cross_context, w_cross_out)
    normed_three = norm_rows(middle_two, gain_low[2])

    hidden_out, grad_normed_three, grad_gateup, grad_down = feed_forward(
        normed_three, cotangent, w_gateup, w_down
    )
    block_out = (middle_two + hidden_out).astype(bf16)
    back_three, grad_gain_three = norm_back(grad_normed_three, middle_two, gain_low[2])
    grad_middle_two = cotangent.astype(f32) + back_three

    cross_branch = grad_middle_two.astype(bf16)
    grad_cross_out = mm_tn(cross_context, cross_branch).astype(bf16)
    grad_cross_context = mm_nt(cross_branch, w_cross_out).astype(bf16)
    grad_cross_queries, part_mk, part_mv = attn_bwd(
        cross_queries, memory_keys, memory_values, cross_probs, grad_cross_context, False, width
    )
    grad_memory_kv = lax.psum_scatter(
        jnp.concatenate([part_mk, part_mv], axis=1), "tp", scatter_dimension=0, tiled=True
    )
    kv_wide = part_mk.shape[1]
    grad_cross_query = mm_tn(normed_cross, grad_cross_queries).astype(bf16)
    grad_normed_cross = mm_nt(grad_cross_queries, w_cross_query)
    grad_cross_keyval = jnp.stack(
        [
            mm_tn(memory, grad_memory_kv[:, :kv_wide]).astype(bf16),
            mm_tn(memory, grad_memory_kv[:, kv_wide:]).astype(bf16),
        ]
    )
    grad_memory = mm_nt(grad_memory_kv[:, :kv_wide], w_cross_keyval[0]) + mm_nt(
        grad_memory_kv[:, kv_wide:], w_cross_keyval[1]
    )
    back_cross, grad_gain_cross = norm_back(grad_normed_cross, middle, gain_low[1])
    grad_middle = grad_middle_two + back_cross

    branch = grad_middle.astype(bf16)
    grad_out = mm_tn(context, branch).astype(bf16)
    grad_context = mm_nt(branch, w_out).astype(bf16)
    grad_queries, part_k, part_v, diagonals = attn_bwd(
        queries, keys, values, probs, grad_context, True, width
    )
    grad_keyvals = lax.psum_scatter(
        jnp.concatenate([part_k, part_v], axis=1), "tp", scatter_dimension=0, tiled=True
    )
    grad_table = jnp.dot(
        diagonals.reshape(-1, width), diag_onehot, precision=lax.Precision.HIGHEST
    )
    grad_query = mm_tn(normed, grad_queries).astype(bf16)
    grad_keyval = jnp.stack(
        [
            mm_tn(normed, grad_keyvals[:, :kv_wide]).astype(bf16),
            mm_tn(normed, grad_keyvals[:, kv_wide:]).astype(bf16),
        ]
    )
    grad_normed = (
        mm_nt(grad_queries, w_query)
        + mm_nt(grad_keyvals[:, :kv_wide], w_keyval[0])
        + mm_nt(grad_keyvals[:, kv_wide:], w_keyval[1])
    )
    back_one, grad_gain_one = norm_back(grad_normed, residual, gain_low[0])
    grad_rows = grad_middle + back_one

    reduced = (
        scatter_sum(grad_query, 0, 1),
        scatter_sum(grad_keyval, 1, 2),
        scatter_sum(grad_out, 1, 0),
        scatter_sum(grad_cross_query, 0, 1),
        scatter_sum(grad_cross_keyval, 1, 2),
        scatter_sum(grad_cross_out, 1, 0),
        scatter_sum(grad_gateup, 2, 0)[0],
        scatter_sum(grad_down, 1, 0),
    )
    squares = jnp.zeros((), f32)
    for piece in reduced:
        squares = squares + jnp.sum(piece * piece)
    gain_terms = jnp.stack([grad_gain_one, grad_gain_cross, grad_gain_three])
    squares_all, gains_full, table_full = lax.psum((squares, gain_terms, grad_table), ("dp", "tp"))
    grad_norm = jnp.sqrt(
        squares_all + jnp.sum(gains_full * gains_full) + jnp.sum(table_full * table_full)
    )
    factor = clip_limit / jnp.maximum(grad_norm, clip_limit)
    gains_grad = lax.dynamic_slice_in_dim(
        gains_full, lax.axis_index("dp") * gains.shape[1], gains.shape[1], 1
    )
    table_grad = lax.dynamic_slice(
        table_full,
        (
            lax.axis_index("tp") * rel_table.shape[0],
            lax.axis_index("dp") * rel_table.shape[1],
        ),
        rel_table.shape,
    )
    grad_list = reduced + (gains_grad, table_grad)
    params = (
        query_w,
        keyval_w,
        out_w,
        cross_query_w,
        cross_keyval_w,
        cross_out_w,
        gateup_w,
        down_w,
        gains,
        rel_table,
    )
    firsts = (
        query_m,
        keyval_m,
        out_m,
        cross_query_m,
        cross_keyval_m,
        cross_out_m,
        gateup_m,
        down_m,
        gains_m,
        rel_table_m,
    )
    seconds = (
        query_v,
        keyval_v,
        out_v,
        cross_query_v,
        cross_keyval_v,
        cross_out_v,
        gateup_v,
        down_v,
        gains_v,
        rel_table_v,
    )
    rates = update_rates()
    new_firsts = []
    new_seconds = []
    new_weights = []
    for position in range(10):
        decay_now = decay_rate if position < 8 else 0.0
        first_new, second_new, weight_new = adam_update(
            params[position],
            grad_list[position],
            firsts[position],
            seconds[position],
            factor,
            decay_now,
            rates[position],
        )
        new_firsts.append(first_new)
        new_seconds.append(second_new)
        new_weights.append(weight_new)
    return (
        block_out,
        grad_rows,
        grad_memory,
        grad_norm,
        new_firsts[0],
        new_firsts[1],
        new_firsts[2],
        new_firsts[3],
        new_firsts[4],
        new_firsts[5],
        new_firsts[6],
        new_firsts[7],
        new_firsts[8],
        new_firsts[9],
        new_seconds[0],
        new_seconds[1],
        new_seconds[2],
        new_seconds[3],
        new_seconds[4],
        new_seconds[5],
        new_seconds[6],
        new_seconds[7],
        new_seconds[8],
        new_seconds[9],
        new_weights[0],
        new_weights[1],
        new_weights[2],
        new_weights[3],
        new_weights[4],
        new_weights[5],
        new_weights[6],
        new_weights[7],
        new_weights[8],
        new_weights[9],
    )


def solution(mesh):
    return jax.shard_map(
        per_device,
        mesh=mesh,
        in_specs=(
            P(("dp", "tp"), None),
            P(("dp", "tp"), None),
            P("dp"),
            P("dp"),
            P(("dp", "tp"), None),
            P("dp", "tp"),
            P(None, "dp", "tp"),
            P("tp", "dp"),
            P("dp", "tp"),
            P(None, "dp", "tp"),
            P("tp", "dp"),
            P(None, "dp", "tp"),
            P("tp", "dp"),
            P(None, "dp"),
            P("tp", "dp"),
            P("dp", "tp"),
            P(None, "dp", "tp"),
            P("tp", "dp"),
            P("dp", "tp"),
            P(None, "dp", "tp"),
            P("tp", "dp"),
            P(None, "dp", "tp"),
            P("tp", "dp"),
            P(None, "dp"),
            P("tp", "dp"),
            P("dp", "tp"),
            P(None, "dp", "tp"),
            P("tp", "dp"),
            P("dp", "tp"),
            P(None, "dp", "tp"),
            P("tp", "dp"),
            P(None, "dp", "tp"),
            P("tp", "dp"),
            P(None, "dp"),
            P("tp", "dp"),
        ),
        out_specs=(
            P(("dp", "tp"), None),
            P(("dp", "tp"), None),
            P(("dp", "tp"), None),
            P(),
            P("dp", "tp"),
            P(None, "dp", "tp"),
            P("tp", "dp"),
            P("dp", "tp"),
            P(None, "dp", "tp"),
            P("tp", "dp"),
            P(None, "dp", "tp"),
            P("tp", "dp"),
            P(None, "dp"),
            P("tp", "dp"),
            P("dp", "tp"),
            P(None, "dp", "tp"),
            P("tp", "dp"),
            P("dp", "tp"),
            P(None, "dp", "tp"),
            P("tp", "dp"),
            P(None, "dp", "tp"),
            P("tp", "dp"),
            P(None, "dp"),
            P("tp", "dp"),
            P("dp", "tp"),
            P(None, "dp", "tp"),
            P("tp", "dp"),
            P("dp", "tp"),
            P(None, "dp", "tp"),
            P("tp", "dp"),
            P(None, "dp", "tp"),
            P("tp", "dp"),
            P(None, "dp"),
            P("tp", "dp"),
        ),
        check_vma=False,
    )
```

time: 2140 us -> 1250 us (0.58); the launches traced: 2100 us -> 1240 us
  local copies, waits for them, and re-layouts: 867 us -> 59.8 us
  matrix products: 143 us -> 47.7 us
  Pallas kernels: 0 us -> 76.4 us
  blocking collectives: 131 us -> 188 us
  other arithmetic: 100 us -> 44.6 us
  loops' own time: 48.2 us -> 0 us
    rev x6 -> x0, local copies, waits for them, and re-layouts: 406 us -> none  [the longest x4 271 us: toeplitz_bias(): return jnp.flip(shifted, axis=2)]
    unnamed x22 -> x35, waiting for transfers between devices: 2.36 us -> 227 us
    while x42 -> x0, local copies, waits for them, and re-layouts: 214 us -> none
    psum x1 -> x0, waiting for transfers between devices: 129 us -> none  [per_device(): lax.psum(jnp.einsum('lh,dh->ld', grad_cross_queries, w_cross_query, prefe...]
    another operation x22 -> x0, local copies, waits for them, and re-layouts: 92.7 us -> none  [the longest x8 91.2 us: toeplitz_bias(): tiled = jnp.tile(strip, (1, block_rows + 1))[:, :block_rows * (width + 1)]]
    dot_general x53 -> x26, matrix products: 140 us -> 47.7 us  [the longest x17 26.7 us: dotf(): return lax.dot_general(a, b, (dims, ((), ())), preferred_element_type=f32)]
    slice x17 -> x1, local copies, waits for them, and re-layouts: 87.2 us -> 0.01 us  [per_device(): normed_three = norm_rows(middle_two, gain_low[2])]
    pallas_call x0 -> x5, Pallas kernels: none -> 76.4 us  [the longest x2 29.5 us: attn_bwd(): pl.pallas_call(functools.partial(bwd_kernel, causal, groups), grid=(pairs...]
  transfers between devices with their start and end apart: 22 -> 29, of which waited for: 13 -> 25; matrix products, arithmetic and copies ran while one was open for 34% -> 9% of each run, Pallas kernels for 0% -> 4%
where the time goes in v1:
time: 1250 us; the launch traced here: 1240 us
  waiting for transfers between devices  800 us (64%)
  blocking collectives  188 us (15%)
  Pallas kernels  76.4 us (6%)
  local copies, waits for them, and re-layouts  59.8 us (5%)
  matrix products  47.7 us (4%)
  other arithmetic  44.6 us (4%)
  between operations  25.1 us (2%)
    unnamed x35, waiting for transfers between devices  227 us
    reduce_scatter x4, waiting for transfers between devices, scatter_sum(): part = lax.psum_scatter(whole, 'dp', scatter_dimension=dp_axis, tiled=True)  210 us
    all_gather x8, waiting for transfers between devices, gather_full(): return lax.all_gather(part, 'dp', axis=dp_axis, tiled=True)  202 us
    all_gather x8, blocking collectives, gather_full(): part = lax.all_gather(shard, 'tp', axis=tp_axis, tiled=True)  130 us
    reduce_scatter x6, waiting for transfers between devices, scatter_sum(): lax.psum_scatter(part, 'tp', scatter_dimension=tp_axis, tiled=True)  125 us
    unnamed x186, local copies, waits for them, and re-layouts  57.1 us
    psum x1, blocking collectives, per_device(): lax.psum((squares, gain_terms, grad_table), ('dp', 'tp'))  39.9 us
    pallas_call x2, Pallas kernels, attn_bwd(): pl.pallas_call(functools.partial(bwd_kernel, causal, groups), grid=(pairs...  29.5 us
  transfers between devices with their start and end apart: 29, of which 25 were waited for; matrix products, arithmetic and copies ran while one was open for 9% of the time, Pallas kernels for 4%

profile of v1, /device:TPU:0, one launch (start us, length us, event | category | flops | bytes accessed | tf_op | source)
XLA Modules:
  0.0 1242.4 jit_solution(16360407157525405194)
XLA Ops:
  28.4 19.5 %all_gather.67 = bf16[2,128,512]{2,1,0:T(8,128)(2,1)} all-gather(bf16[2,128,128]{2,1,0:T(8,128)(2,1)S(1)} %convert_element_type.162), channel_id=1, replica_groups=mesh['dp'=8,'tp'=4] {'tp'}, dimensions={2}, use_global_device_ids=true | all-gather | bytes 327680 | tf_op jit(solution)/shard_map/all_gather | solution.py:256
  81.1 17.5 %all_gather.73 = bf16[128,1024]{1,0:T(8,128)(2,1)} all-gather(bf16[128,256]{1,0:T(8,128)(2,1)S(1)} %convert_element_type.171), channel_id=1, replica_groups=mesh['dp'=8,'tp'=4] {'tp'}, dimensions={1}, use_global_device_ids=true | all-gather | bytes 327680 | tf_op jit(solution)/shard_map/all_gather | solution.py:256
  208.7 26.0 %all-gather.25.cloned.1.call-done = bf16[512,1024]{1,0:T(8,128)(2,1)} async-done(((bf16[128,1024]{1,0:T(8,128)(2,1)}), bf16[512,1024]{1,0:T(8,128)(2,1)}) %all-gather.25.cloned.1.call-update) | async-done | bytes 1048592 | tf_op jit(solution)/shard_map/all_gather | solution.py:326
  234.7 29.3 %all-gather.27.cloned.1.call-done = bf16[2,1024,512]{2,1,0:T(8,128)(2,1)} async-done(((bf16[2,128,512]{2,1,0:T(8,128)(2,1)}), bf16[2,1024,512]{2,1,0:T(8,128)(2,1)}) %all-gather.27.cloned.1.call-update) | async-done | bytes 2097168 | tf_op jit(solution)/shard_map/all_gather | solution.py:257
  268.7 25.1 %all-gather.23.cloned.1.call-done = bf16[1024,1024]{1,0:T(8,128)(2,1)} async-done(((bf16[128,1024]{1,0:T(8,128)(2,1)}), bf16[1024,1024]{1,0:T(8,128)(2,1)}) %all-gather.23.cloned.1.call-update) | async-done | bytes 2097168 | tf_op jit(solution)/shard_map/all_gather | solution.py:257
  328.7 41.4 %all-gather.33.cloned.1.call-done.wd_ref = bf16[2816,1024]{1,0:T(8,128)(2,1)} async-done(((bf16[2816,128]{1,0:T(8,128)(2,1)}), bf16[2816,1024]{1,0:T(8,128)(2,1)}) %all-gather.33.cloned.1.call-update) | async-done | bytes 5767184 | tf_op jit(solution)/shard_map/all_gather | solution.py:257
  370.1 74.1 %all-gather.31.cloned.1.call-done.wg_ref = bf16[4,2,1024,704]{3,2,1,0:T(8,128)(2,1)} async-done(((bf16[4,2,128,704]{3,2,1,0:T(8,128)(2,1)}), bf16[4,2,1024,704]{3,2,1,0:T(8,128)(2,1)}) %all-gather.31.cloned.1.call-update) | async-done | bytes 11534352 | tf_op jit(solution)/shard_map/all_gather | solution.py:257
  444.1 22.3 %feed_forward.1 = (f32[256,1024]{1,0:T(8,128)}, f32[256,1024]{1,0:T(8,128)}, bf16[4,2,1024,704]{3,2,1,0:T(8,128)(2,1)}, bf16[2816,1024]{1,0:T(8,128)(2,1)}) custom-call(bf16[256,1024]{1,0:T(8,128)(2,1)} %multiply_convert_fusion.x_ref, bf16[256,1024]{1,0:T(8,128)(2,1)} %c_ref.1, bf16[4,2,1024,704]{3,2,1,0:T(8,128)(2,1)} %all-gather.31.cloned.1.call-done.wg_ref, ...), custom_call_target="tpu_custom_call" | custom-call | tf_op jit(solution)/shard_map/feed_forward/pallas_call | solution.py:227
  490.5 19.3 %attend_bwd.3 = (bf16[256,1024]{1,0:T(8,128)(2,1)S(1)}, bf16[1024,512]{1,0:T(8,128)(2,1)S(1)}, bf16[1024,512]{1,0:T(8,128)(2,1)S(1)}, f32[4,4,1280]{2,1,0:T(4,128)S(1)}) custom-call(bf16[256,1024]{1,0:T(8,128)(2,1)S(1)} %copy-done.11, bf16[1024,512]{1,0:T(8,128)(2,1)S(1)} %convolution_convert_fusion.9.k_ref, ...), custom_call_target="tpu_custom_call" | custom-call | tf_op jit(solution)/shard_map/attend_bwd/pallas_call | solution.py:158
  570.4 30.0 %reduce-scatter.43.cloned.1.call-done = bf16[128,1024]{1,0:T(8,128)(2,1)} async-done(((bf16[1024,1024]{1,0:T(8,128)(2,1)}), bf16[128,1024]{1,0:T(8,128)(2,1)}) %reduce-scatter.43.cloned.1.call-update) | async-done | bytes 262160 | tf_op jit(solution)/shard_map/reduce_scatter | solution.py:261
  600.4 44.7 %reduce-scatter.35.cloned.1.call-done = bf16[128,1024]{1,0:T(8,128)(2,1)} async-done(((bf16[1024,1024]{1,0:T(8,128)(2,1)}), bf16[128,1024]{1,0:T(8,128)(2,1)}) %reduce-scatter.35.cloned.1.call-update) | async-done | bytes 262160 | tf_op jit(solution)/shard_map/reduce_scatter | solution.py:261
  645.2 44.3 %reduce-scatter.57.cloned.1.call-done = bf16[128,1024]{1,0:T(8,128)(2,1)} async-done(((bf16[1024,1024]{1,0:T(8,128)(2,1)}), bf16[128,1024]{1,0:T(8,128)(2,1)}) %reduce-scatter.57.cloned.1.call-update) | async-done | bytes 262160
  691.3 42.9 %reduce-scatter.63.cloned.1.call-done = bf16[128,1024]{1,0:T(8,128)(2,1)} async-done(((bf16[1024,1024]{1,0:T(8,128)(2,1)}), bf16[128,1024]{1,0:T(8,128)(2,1)}) %reduce-scatter.63.cloned.1.call-update) | async-done | bytes 262160
  736.1 42.5 %reduce-scatter.59.cloned.1.call-done = bf16[128,1024]{1,0:T(8,128)(2,1)} async-done(((bf16[1024,1024]{1,0:T(8,128)(2,1)}), bf16[128,1024]{1,0:T(8,128)(2,1)}) %reduce-scatter.59.cloned.1.call-update) | async-done | bytes 262160
  781.0 42.5 %reduce-scatter.39.cloned.1.call-done = bf16[2,128,512]{2,1,0:T(8,128)(2,1)} async-done(((bf16[2,1024,512]{2,1,0:T(8,128)(2,1)}), bf16[2,128,512]{2,1,0:T(8,128)(2,1)}) %reduce-scatter.39.cloned.1.call-update) | async-done | bytes 262160 | tf_op jit(solution)/shard_map/reduce_scatter | solution.py:261
  825.4 60.5 %reduce-scatter.65.cloned.1.call-done = bf16[128,2816]{1,0:T(8,128)(2,1)} async-done(((bf16[1024,2816]{1,0:T(8,128)(2,1)}), bf16[128,2816]{1,0:T(8,128)(2,1)}) %reduce-scatter.65.cloned.1.call-update) | async-done | bytes 720912
  889.4 92.8 %reduce-scatter.49.cloned.1.call-done = bf16[4,2,128,704]{3,2,1,0:T(8,128)(2,1)} async-done(((bf16[4,2,1024,704]{3,2,1,0:T(8,128)(2,1)}), bf16[4,2,128,704]{3,2,1,0:T(8,128)(2,1)}) %reduce-scatter.49.cloned.1.call-update) | async-done | bytes 1441808 | tf_op jit(solution)/shard_map/reduce_scatter | solution.py:261
  1005.7 18.7 %reduce-scatter.37.cloned.1.call-done = bf16[128,256]{1,0:T(8,128)(2,1)} async-done(((bf16[128,1024]{1,0:T(8,128)(2,1)}), bf16[128,256]{1,0:T(8,128)(2,1)}) %reduce-scatter.37.cloned.1.call-update) | async-done | bytes 65552 | tf_op jit(solution)/shard_map/reduce_scatter | solution.py:262
  1025.9 19.3 %reduce-scatter.41.cloned.1.call-done = bf16[256,128]{1,0:T(8,128)(2,1)} async-done(((bf16[1024,128]{1,0:T(8,128)(2,1)}), bf16[256,128]{1,0:T(8,128)(2,1)}) %reduce-scatter.41.cloned.1.call-update) | async-done | bytes 65552 | tf_op jit(solution)/shard_map/reduce_scatter | solution.py:262
  1046.6 19.3 %reduce-scatter.47.cloned.1.call-done = bf16[256,128]{1,0:T(8,128)(2,1)} async-done(((bf16[1024,128]{1,0:T(8,128)(2,1)}), bf16[256,128]{1,0:T(8,128)(2,1)}) %reduce-scatter.47.cloned.1.call-update) | async-done | bytes 65552 | tf_op jit(solution)/shard_map/reduce_scatter | solution.py:262
  1088.2 19.0 %reduce-scatter.55.cloned.1.call-done = bf16[128,256]{1,0:T(8,128)(2,1)} async-done(((bf16[512,256]{1,0:T(8,128)(2,1)}), bf16[128,256]{1,0:T(8,128)(2,1)}) %reduce-scatter.55.cloned.1.call-update) | async-done | bytes 65552
  1112.7 18.5 %reduce-scatter.53.cloned.1.call-done = bf16[704,128]{1,0:T(8,128)(2,1)} async-done(((bf16[2816,128]{1,0:T(8,128)(2,1)}), bf16[704,128]{1,0:T(8,128)(2,1)}) %reduce-scatter.53.cloned.1.call-update) | async-done | bytes 180240 | tf_op jit(solution)/shard_map/reduce_scatter | solution.py:262
  1132.8 35.1 %reduce-scatter.51.cloned.1.call-done = bf16[1,2,128,704]{3,2,1,0:T(8,128)(2,1)} async-done(((bf16[4,2,128,704]{3,2,1,0:T(8,128)(2,1)}), bf16[1,2,128,704]{3,2,1,0:T(8,128)(2,1)}) %reduce-scatter.51.cloned.1.call-update) | async-done | bytes 360464 | tf_op jit(solution)/shard_map/reduce_scatter | solution.py:262
  1173.6 39.9 %all-reduce = (f32[]{:T(128)}, f32[3,1024]{1,0:T(4,128)S(1)}, f32[16,32]{1,0:T(8,128)S(1)}) all-reduce(f32[]{:T(128)S(6)} %add.319, f32[3,1024]{1,0:T(4,128)S(1)} %pad_maximum_fusion.4, f32[16,32]{1,0:T(8,128)S(1)} %fusion.24), channel_id=1, replica_groups=mesh['dp'=8,'tp'=4] {'dp','tp'}, use_global_device_ids=true, to_apply=%region_34.35 | all-reduce | flops 3585 | bytes 28680 | tf_op jit(solution)/shard_map/psum | solution.py:433
  (350 shorter events, 373.0 us)
Async XLA Ops:
  9.3 155.9 %all-gather.17.cloned.1.call-start = ((), (), s32[]{:S(2)}) async-start(), calls=%async_computation.19 | async-start | bytes 2621440 | tf_op jit(solution)/shard_map/all_gather | solution.py:325
  10.1 157.6 %all-gather.15.cloned.1.call-start = ((), (), s32[]{:S(2)}) async-start(), calls=%async_computation.18 | async-start | bytes 2359296 | tf_op jit(solution)/shard_map/all_gather | solution.py:257
  47.9 157.4 %all-gather.21.cloned.1.call-start = ((), (), s32[]{:S(2)}) async-start(), calls=%async_computation.21 | async-start | bytes 2359296 | tf_op jit(solution)/shard_map/all_gather | solution.py:257
  64.4 170.3 %all-gather.25.cloned.1.call-start = ((), (), s32[]{:S(2)}) async-start(), calls=%async_computation.23 | async-start | bytes 1310720 | tf_op jit(solution)/shard_map/all_gather | solution.py:326
  65.0 199.0 %all-gather.27.cloned.1.call-start = ((), (), s32[]{:S(2)}) async-start(), calls=%async_computation.24 | async-start | bytes 2359296 | tf_op jit(solution)/shard_map/all_gather | solution.py:257
  81.0 212.8 %all-gather.23.cloned.1.call-start = ((), (), s32[]{:S(2)}) async-start(), calls=%async_computation.22 | async-start | bytes 2359296 | tf_op jit(solution)/shard_map/all_gather | solution.py:257
  98.6 225.3 %all-gather.29.cloned.1.call-start = ((), (), s32[]{:S(2)}) async-start(), calls=%async_computation.25 | async-start | bytes 2359296 | tf_op jit(solution)/shard_map/all_gather | solution.py:257
  115.8 254.3 %all-gather.33.cloned.1.call-start = ((), (), s32[]{:S(2)}) async-start(), calls=%async_computation.27 | async-start | bytes 6488064 | tf_op jit(solution)/shard_map/all_gather | solution.py:257
  132.2 311.9 %all-gather.31.cloned.1.call-start = ((), (), s32[]{:S(2)}) async-start(), calls=%async_computation.26 | async-start | bytes 14155776 | tf_op jit(solution)/shard_map/all_gather | solution.py:257
  134.9 397.2 %reduce-scatter.33.cloned.1.call-start = ((), (), s32[]{:S(2)}) async-start(), calls=%async_computation.29 | async-start | bytes 1310720 | tf_op jit(solution)/shard_map/reduce_scatter | solution.py:374
  518.1 171.4 %reduce-scatter.57.cloned.1.call-start = ((), (), s32[]{:S(2)}) async-start(), calls=%async_computation.42 | async-start | bytes 2359296
  524.6 209.6 %reduce-scatter.63.cloned.1.call-start = ((), (), s32[]{:S(2)}) async-start(), calls=%async_computation.45 | async-start | bytes 2359296
  532.0 246.6 %reduce-scatter.59.cloned.1.call-start = ((), (), s32[]{:S(2)}) async-start(), calls=%async_computation.43 | async-start | bytes 2359296
  546.9 276.6 %reduce-scatter.39.cloned.1.call-start = ((), (), s32[]{:S(2)}) async-start(), calls=%async_computation.32 | async-start | bytes 2359296 | tf_op jit(solution)/shard_map/reduce_scatter | solution.py:261
  561.2 324.6 %reduce-scatter.65.cloned.1.call-start = ((), (), s32[]{:S(2)}) async-start(), calls=%async_computation.46 | async-start | bytes 6488064
  569.6 412.6 %reduce-scatter.49.cloned.1.call-start = ((), (), s32[]{:S(2)}) async-start(), calls=%async_computation.37 | async-start | bytes 14155776 | tf_op jit(solution)/shard_map/reduce_scatter | solution.py:261
  570.3 433.9 %reduce-scatter.45.cloned.1.call-start = ((), (), s32[]{:S(2)}) async-start(), calls=%async_computation.35 | async-start | bytes 327680 | tf_op jit(solution)/shard_map/reduce_scatter | solution.py:262
  600.4 424.0 %reduce-scatter.37.cloned.1.call-start = ((), (), s32[]{:S(2)}) async-start(), calls=%async_computation.31 | async-start | bytes 327680 | tf_op jit(solution)/shard_map/reduce_scatter | solution.py:262
  645.1 400.0 %reduce-scatter.41.cloned.1.call-start = ((), (), s32[]{:S(2)}) async-start(), calls=%async_computation.33 | async-start | bytes 327680 | tf_op jit(solution)/shard_map/reduce_scatter | solution.py:262
  691.3 374.6 %reduce-scatter.47.cloned.1.call-start = ((), (), s32[]{:S(2)}) async-start(), calls=%async_computation.36 | async-start | bytes 327680 | tf_op jit(solution)/shard_map/reduce_scatter | solution.py:262
  736.0 350.5 %reduce-scatter.61.cloned.1.call-start = ((), (), s32[]{:S(2)}) async-start(), calls=%async_computation.44 | async-start | bytes 327680
  780.9 326.3 %reduce-scatter.55.cloned.1.call-start = ((), (), s32[]{:S(2)}) async-start(), calls=%async_computation.41 | async-start | bytes 327680
  825.3 305.8 %reduce-scatter.53.cloned.1.call-start = ((), (), s32[]{:S(2)}) async-start(), calls=%async_computation.39 | async-start | bytes 901120 | tf_op jit(solution)/shard_map/reduce_scatter | solution.py:262
  888.1 279.8 %reduce-scatter.51.cloned.1.call-start = ((), (), s32[]{:S(2)}) async-start(), calls=%async_computation.38 | async-start | bytes 1966080 | tf_op jit(solution)/shard_map/reduce_scatter | solution.py:262
  (86 other events, 1719.9 us)
Sparse Core Ops, SparseCore 0:
  10.2 45.8 all-gather.34
  57.7 59.7 all-gather.16
  119.4 26.2 all-gather.14
  147.4 27.9 all-gather.18
  177.1 28.1 all-gather.20
  206.7 27.9 all-gather.24
  236.6 27.3 all-gather.26
  265.9 27.8 all-gather.22
  295.7 28.1 all-gather.28
  325.7 44.3 all-gather.32
  372.0 72.1 all-gather.30
  484.5 27.1 reduce-scatter.32
  514.1 42.4 reduce-scatter.30
  559.8 40.5 reduce-scatter.42
  603.8 41.2 reduce-scatter.34
  648.2 41.1 reduce-scatter.56
  692.9 41.2 reduce-scatter.62
  737.3 41.1 reduce-scatter.58
  782.2 41.2 reduce-scatter.38
  826.8 59.0 reduce-scatter.64
  889.8 92.3 reduce-scatter.48
  984.5 19.6 reduce-scatter.44
  1110.1 21.0 reduce-scatter.52
  1133.6 34.2 reduce-scatter.50
  (5 shorter events, 89.1 us)

commit v2 on v1

--- a/solution.py
+++ b/solution.py
@@ -160,6 +160,522 @@
     return r
 
 
+MESH = pl.DeviceIdType.MESH
+
+
+def neighbour(kind):
+    dp = lax.axis_index("dp")
+    tp = lax.axis_index("tp")
+    if kind == "core":
+        return (dp ^ 1, tp)
+    if kind == "x":
+        return (dp ^ 2, tp)
+    if kind == "y":
+        return (dp ^ 4, tp)
+    if kind == "up":
+        return (dp, tp + 1)
+    if kind == "down":
+        return (dp, tp - 1)
+
+
+class Row:
+    def __init__(self, lead, dp_part, tp_part, tp_size):
+        self.lead = lead
+        self.dp_part = dp_part
+        self.tp_part = tp_part
+        self.full = lead + (dp_part * 8, tp_part * tp_size)
+        self.slab_shape = lead + (dp_part, tp_part * tp_size)
+        self.shard = lead + (dp_part, tp_part)
+        self.half_shape = lead + (dp_part, tp_part * (tp_size // 2))
+        self.tp_size = tp_size
+
+    def index(self, start, count):
+        return (slice(None),) * len(self.lead) + (
+            slice(None),
+            pl.ds(pl.multiple_of(start * self.tp_part, self.tp_part), count * self.tp_part),
+        )
+
+    def one(self, start):
+        return self.index(start, 1)
+
+    def of(self, ref, dp):
+        rows = pl.ds(pl.multiple_of(dp * self.dp_part, self.dp_part), self.dp_part)
+        return ref.at[(slice(None),) * len(self.lead) + (rows, slice(None))]
+
+    def part(self, ref, dp, start, count):
+        rows = pl.ds(pl.multiple_of(dp * self.dp_part, self.dp_part), self.dp_part)
+        cols = pl.ds(pl.multiple_of(start * self.tp_part, self.tp_part), count * self.tp_part)
+        return ref.at[(slice(None),) * len(self.lead) + (rows, cols)]
+
+
+class Column:
+    def __init__(self, dp_part, tp_part, tp_size):
+        self.dp_part = dp_part
+        self.tp_part = tp_part
+        self.full = (tp_part * tp_size, dp_part * 8)
+        self.slab_shape = (tp_part * tp_size, dp_part)
+        self.shard = (tp_part, dp_part)
+        self.half_shape = (tp_part * (tp_size // 2), dp_part)
+        self.tp_size = tp_size
+
+    def index(self, start, count):
+        return (
+            pl.ds(pl.multiple_of(start * self.tp_part, self.tp_part), count * self.tp_part),
+            slice(None),
+        )
+
+    def one(self, start):
+        return self.index(start, 1)
+
+    def of(self, ref, dp):
+        return self.part(ref, dp, 0, self.tp_size)
+
+    def part(self, ref, dp, start, count):
+        cols = pl.ds(pl.multiple_of(dp * self.dp_part, self.dp_part), self.dp_part)
+        rows = pl.ds(pl.multiple_of(start * self.tp_part, self.tp_part), count * self.tp_part)
+        return ref.at[rows, cols]
+
+
+class Block:
+    def __init__(self, dp_part, tp_part, tp_size):
+        self.dp_part = dp_part
+        self.full = (tp_size, dp_part * 8, tp_part)
+        self.slab_shape = (tp_size, dp_part, tp_part)
+        self.shard = (dp_part, tp_part)
+        self.half_shape = (tp_size // 2, dp_part, tp_part)
+        self.tp_size = tp_size
+
+    def index(self, start, count):
+        return (pl.ds(start, count),)
+
+    def one(self, start):
+        return (start,)
+
+    def of(self, ref, dp):
+        return self.part(ref, dp, 0, self.tp_size)
+
+    def part(self, ref, dp, start, count):
+        rows = pl.ds(pl.multiple_of(dp * self.dp_part, self.dp_part), self.dp_part)
+        return ref.at[start if count == 1 else pl.ds(start, count), rows]
+
+
+def when(condition, action):
+    pl.when(condition)(action)
+
+
+def copy_to(src, dst, send_sem, recv_sem, kind):
+    return pltpu.make_async_remote_copy(
+        src, dst, send_sem, recv_sem, device_id=neighbour(kind), device_id_type=MESH
+    )
+
+
+def greet(tp_size, reach):
+    dp = lax.axis_index("dp")
+    tp = lax.axis_index("tp")
+    barrier = pltpu.get_barrier_semaphore()
+    for kind in ("core", "x", "y"):
+        pl.semaphore_signal(barrier, inc=1, device_id=neighbour(kind), device_id_type=MESH)
+
+    peers = 3
+    for d in range(1, reach + 1):
+        above = tp + d < tp_size
+        below = tp >= d
+
+        @pl.when(above)
+        def _(d=d):
+            pl.semaphore_signal(barrier, inc=1, device_id=(dp, tp + d), device_id_type=MESH)
+
+        @pl.when(below)
+        def _(d=d):
+            pl.semaphore_signal(barrier, inc=1, device_id=(dp, tp - d), device_id_type=MESH)
+
+        peers = peers + above.astype(jnp.int32) + below.astype(jnp.int32)
+
+    pl.semaphore_wait(barrier, peers)
+
+
+def gather_kernel(specs, plane, tp_size, *refs):
+    count = len(specs)
+    ins = refs[:count]
+    outs = refs[count : 2 * count]
+    local_sem, z_send, z_recv, p_send, p_recv = refs[2 * count :]
+    dp = lax.axis_index("dp")
+    tp = lax.axis_index("tp")
+    greet(tp_size, 2)
+
+    def own(k):
+        return pltpu.make_async_copy(ins[k], specs[k].part(outs[k], dp, tp, 1), local_sem.at[k])
+
+    def way(k, d, sign):
+        slot = 0 if sign > 0 else 1
+        return pltpu.make_async_remote_copy(
+            ins[k],
+            specs[k].part(outs[k], dp, tp, 1),
+            z_send.at[k, slot, d - 1],
+            z_recv.at[k, slot, d - 1],
+            device_id=(dp, tp + sign * d),
+            device_id_type=MESH,
+        )
+
+    def onward(k, sign):
+        slot = 0 if sign > 0 else 1
+        piece = specs[k].part(outs[k], dp, tp - 2 * sign, 1)
+        return pltpu.make_async_remote_copy(
+            piece,
+            piece,
+            z_send.at[k, slot, 2],
+            z_recv.at[k, slot, 2],
+            device_id=(dp, tp + sign),
+            device_id_type=MESH,
+        )
+
+    def has(d, sign):
+        return (tp + d < tp_size) if sign > 0 else (tp >= d)
+
+    def z_start(k):
+        own(k).start()
+        for sign in (1, -1):
+            for d in (2, 1):
+                when(has(d, sign), lambda d=d, sign=sign: way(k, d, sign).start())
+
+    def relays(sign):
+        return has(2, -sign) & has(1, sign)
+
+    def z_relay(k):
+        for sign in (1, -1):
+
+            def act(sign=sign):
+                way(k, 2, sign).wait_recv()
+                onward(k, sign).start()
+
+            when(relays(sign), act)
+
+    def z_wait(k):
+        for sign in (1, -1):
+            when(has(1, -sign), lambda sign=sign: way(k, 1, sign).wait_recv())
+            when(
+                has(2, -sign) & jnp.logical_not(relays(sign)),
+                lambda sign=sign: way(k, 2, sign).wait_recv(),
+            )
+            when(has(3, -sign), lambda sign=sign: onward(k, sign).wait_recv())
+
+    half = tp_size // 2
+
+    def slab(k, who, slot, kind):
+        piece = specs[k].of(outs[k], who)
+        return copy_to(piece, piece, p_send.at[k, slot], p_recv.at[k, slot], kind)
+
+    def halves(k, who, h, slot, kind):
+        piece = specs[k].part(outs[k], who, h * half, half)
+        return copy_to(piece, piece, p_send.at[k, slot], p_recv.at[k, slot], kind)
+
+    def plane_start(k):
+        own(k).wait()
+        z_wait(k)
+        if plane[k]:
+            slab(k, dp, 0, "x").start()
+            slab(k, dp, 1, "y").start()
+            slab(k, dp, 2, "core").start()
+
+    def plane_relay(k):
+        if plane[k]:
+            slab(k, dp ^ 2, 0, "x").wait_recv()
+            halves(k, dp ^ 2, 0, 3, "y").start()
+            slab(k, dp ^ 4, 1, "y").wait_recv()
+            halves(k, dp ^ 4, 1, 4, "x").start()
+            slab(k, dp ^ 2, 5, "core").start()
+            slab(k, dp ^ 4, 6, "core").start()
+
+    def plane_last(k):
+        if plane[k]:
+            halves(k, dp ^ 6, 0, 3, "y").wait_recv()
+            halves(k, dp ^ 6, 0, 7, "core").start()
+            halves(k, dp ^ 6, 1, 4, "x").wait_recv()
+            halves(k, dp ^ 6, 1, 8, "core").start()
+
+    def finish(k):
+        for sign in (1, -1):
+            for d in (1, 2):
+                when(has(d, sign), lambda d=d, sign=sign: way(k, d, sign).wait_send())
+            when(relays(sign), lambda sign=sign: onward(k, sign).wait_send())
+        if plane[k]:
+            slab(k, dp, 0, "x").wait_send()
+            slab(k, dp, 1, "y").wait_send()
+            slab(k, dp, 2, "core").wait()
+            halves(k, dp ^ 2, 0, 3, "y").wait_send()
+            halves(k, dp ^ 4, 1, 4, "x").wait_send()
+            slab(k, dp ^ 2, 5, "core").wait()
+            slab(k, dp ^ 4, 6, "core").wait()
+            halves(k, dp ^ 6, 0, 7, "core").wait()
+            halves(k, dp ^ 6, 1, 8, "core").wait()
+
+    stages = ((z_start, 0), (z_relay, 1), (plane_start, 2), (plane_relay, 4), (plane_last, 5))
+    for step in range(count + stages[-1][1]):
+        for stage, late in stages:
+            if 0 <= step - late < count:
+                stage(step - late)
+    for k in range(count):
+        finish(k)
+
+
+def gather_all(shards, specs, plane, tp_size):
+    count = len(specs)
+    return pl.pallas_call(
+        functools.partial(gather_kernel, specs, plane, tp_size),
+        in_specs=[pl.BlockSpec(memory_space=pl.ANY)] * count,
+        out_specs=[pl.BlockSpec(memory_space=pl.ANY)] * count,
+        out_shape=[
+            jax.ShapeDtypeStruct(spec.full if flag else spec.slab_shape, shard.dtype)
+            for spec, flag, shard in zip(specs, plane, shards)
+        ],
+        scratch_shapes=[
+            pltpu.SemaphoreType.DMA((count,)),
+            pltpu.SemaphoreType.DMA((count, 2, 3)),
+            pltpu.SemaphoreType.DMA((count, 2, 3)),
+            pltpu.SemaphoreType.DMA((count, 9)),
+            pltpu.SemaphoreType.DMA((count, 9)),
+        ],
+        compiler_params=pltpu.CompilerParams(collective_id=1, has_side_effects=True),
+        name="gather_all",
+    )(*shards)
+
+
+class Rows:
+    def __init__(self, tp_part, columns, tp_size):
+        self.tp_part = tp_part
+        self.slab_shape = (tp_part * tp_size, columns)
+        self.full = self.slab_shape
+        self.shard = (tp_part, columns)
+
+    def part(self, ref, dp, start, count):
+        return ref.at[pl.ds(pl.multiple_of(start * self.tp_part, self.tp_part), count * self.tp_part)]
+
+
+def add_views(dst, dst_index, sources):
+    target = dst.at[dst_index]
+    shape = target.shape
+    lead = shape[:-2]
+    rows = shape[-2]
+    chunk = 64 if rows % 64 == 0 else 16
+    for outer in np.ndindex(*lead):
+
+        def body(i, unused, outer=outer):
+            here = outer + (pl.ds(pl.multiple_of(i * chunk, chunk), chunk), slice(None))
+            total = target[here].astype(f32)
+            for source in sources:
+                total = total + source[here].astype(f32)
+            target[here] = total.astype(bf16)
+            return unused
+
+        lax.fori_loop(0, rows // chunk, body, 0)
+
+
+def reduce_kernel(specs, tp_size, *refs):
+    count = len(specs)
+    ins = refs[:count]
+    small_in = refs[count]
+    outs = refs[count + 1 : 2 * count + 1]
+    small_out = refs[2 * count + 1]
+    norm_out = refs[2 * count + 2]
+    scratch = refs[2 * count + 3 :]
+    own = scratch[0:count]
+    other = scratch[count : 2 * count]
+    half_x = scratch[2 * count : 3 * count]
+    half_y = scratch[3 * count : 4 * count]
+    from_x = scratch[4 * count : 5 * count]
+    from_y = scratch[5 * count : 6 * count]
+    from_z = scratch[6 * count : 7 * count]
+    small_acc, small_got, square_acc, square_all, square_got = scratch[7 * count : 7 * count + 5]
+    load_sem, c_send, c_recv, p_send, p_recv, z_send, z_recv, s_send, s_recv = scratch[7 * count + 5 :]
+    dp = lax.axis_index("dp")
+    tp = lax.axis_index("tp")
+    greet(tp_size, tp_size - 1)
+    half = tp_size // 2
+
+    def load(k, j):
+        return pltpu.make_async_copy(specs[k].of(ins[k], dp ^ (2 * j)), own[k].at[j], load_sem.at[k, j])
+
+    def to_core(k, j):
+        return copy_to(
+            specs[k].of(ins[k], dp ^ (2 * j) ^ 1), other[k].at[j], c_send.at[k, j], c_recv.at[k, j], "core"
+        )
+
+    def start(k):
+        for j in (3, 2, 1, 0):
+            to_core(k, j).start()
+            load(k, j).start()
+
+    def send_half(k, h):
+        piece = own[k].at[(3,) + specs[k].index(h * half, half)]
+        return copy_to(
+            piece, (half_x, half_y)[h][k], p_send.at[k, h], p_recv.at[k, h], ("x", "y")[h]
+        )
+
+    def send_slab(k, j):
+        return copy_to(
+            own[k].at[j],
+            (from_x, from_y)[j - 1][k],
+            p_send.at[k, j + 1],
+            p_recv.at[k, j + 1],
+            ("x", "y")[j - 1],
+        )
+
+    def cores(k):
+        for j in (3, 2, 1, 0):
+            to_core(k, j).wait_recv()
+            load(k, j).wait()
+            add_views(own[k], (j,), [other[k].at[j]])
+            if j == 3:
+                send_half(k, 0).start()
+                send_half(k, 1).start()
+
+    def halves(k):
+        send_half(k, 1).wait_recv()
+        add_views(own[k], (1,) + specs[k].index(half, half), [half_y[k]])
+        send_slab(k, 1).start()
+        send_half(k, 0).wait_recv()
+        add_views(own[k], (2,) + specs[k].index(0, half), [half_x[k]])
+        send_slab(k, 2).start()
+
+    def to_z(k, offset):
+        target = lax.rem(tp + offset, tp_size)
+        piece = own[k].at[(0,) + specs[k].one(target)]
+        return pltpu.make_async_remote_copy(
+            piece,
+            from_z[k].at[offset - 1],
+            z_send.at[k, offset - 1],
+            z_recv.at[k, offset - 1],
+            device_id=(dp, target),
+            device_id_type=MESH,
+        )
+
+    def slabs(k):
+        send_slab(k, 1).wait_recv()
+        send_slab(k, 2).wait_recv()
+        add_views(own[k], (0,), [from_x[k], from_y[k]])
+        for offset in range(1, tp_size):
+            to_z(k, offset).start()
+
+    def last(k):
+        for offset in range(1, tp_size):
+            to_z(k, offset).wait_recv()
+        shape = specs[k].shard
+        lead = shape[:-2]
+        rows = shape[-2]
+        chunk = 64 if rows % 64 == 0 else 16
+        mine = own[k].at[(0,) + specs[k].one(tp)]
+        for outer in np.ndindex(*lead):
+
+            def body(i, squares, outer=outer):
+                here = outer + (pl.ds(pl.multiple_of(i * chunk, chunk), chunk), slice(None))
+                total = mine[here].astype(f32)
+                for offset in range(1, tp_size):
+                    total = total + from_z[k][(offset - 1,) + here].astype(f32)
+                outs[k][here] = total
+                squared = jnp.sum((total * total).reshape(chunk // 8, 8, -1), axis=0)
+                return squares + jnp.sum(squared, axis=1, keepdims=True)
+
+            square_acc[...] += jnp.broadcast_to(
+                lax.fori_loop(0, rows // chunk, body, jnp.zeros((8, 1), f32)), square_acc.shape
+            )
+
+    def exchange(acc, got, base):
+        partners = [(dp ^ 1, tp), (dp ^ 2, tp), (dp ^ 4, tp), (dp, tp ^ 1), (dp, tp ^ 2)]
+
+        def step(i):
+            return pltpu.make_async_remote_copy(
+                acc.at[i],
+                got.at[i],
+                s_send.at[base + i],
+                s_recv.at[base + i],
+                device_id=partners[i],
+                device_id_type=MESH,
+            )
+
+        def run(i):
+            step(i).wait_recv()
+            acc[i + 1] = acc[i] + got[i]
+            if i < 4:
+                step(i + 1).start()
+
+        return step, run
+
+    small_step, small_run = exchange(small_acc, small_got, 0)
+    square_step, square_run = exchange(square_all, square_got, 5)
+    small_acc[0] = small_in[...]
+    small_step(0).start()
+    square_acc[...] = jnp.zeros(square_acc.shape, f32)
+    for k in range(count):
+        start(k)
+    stages = ((cores, 0), (halves, 1), (slabs, 2), (last, 3))
+    for step in range(count + stages[-1][1]):
+        for stage, late in reversed(stages):
+            if 0 <= step - late < count:
+                stage(step - late)
+        if step < 5:
+            small_run(step)
+    small_out[...] = small_acc[5]
+    square_all[0] = square_acc[...]
+    square_step(0).start()
+    for i in range(5):
+        square_run(i)
+    norm_out[...] = square_all[5]
+    for i in range(5):
+        small_step(i).wait_send()
+        square_step(i).wait_send()
+    for k in range(count):
+        for j in range(4):
+            to_core(k, j).wait_send()
+        for h in range(2):
+            send_half(k, h).wait_send()
+            send_slab(k, h + 1).wait_send()
+        for offset in range(1, tp_size):
+            to_z(k, offset).wait_send()
+
+
+def reduce_all(wholes, small, specs, tp_size):
+    count = len(specs)
+    slab = lambda spec, lead: pltpu.VMEM(lead + spec.slab_shape, bf16)
+    part = lambda spec: pltpu.VMEM(spec.half_shape, bf16)
+    scratch = [slab(spec, (4,)) for spec in specs]
+    scratch += [slab(spec, (4,)) for spec in specs]
+    scratch += [part(spec) for spec in specs] * 2
+    scratch += [slab(spec, ()) for spec in specs] * 2
+    scratch += [pltpu.VMEM((tp_size - 1,) + spec.shard, bf16) for spec in specs]
+    scratch += [
+        pltpu.VMEM((6,) + small.shape, f32),
+        pltpu.VMEM((5,) + small.shape, f32),
+        pltpu.VMEM((8, 128), f32),
+        pltpu.VMEM((6, 8, 128), f32),
+        pltpu.VMEM((5, 8, 128), f32),
+    ]
+    sems = lambda *shape: pltpu.SemaphoreType.DMA(shape)
+    scratch += [
+        sems(count, 4),
+        sems(count, 4),
+        sems(count, 4),
+        sems(count, 4),
+        sems(count, 4),
+        sems(count, tp_size - 1),
+        sems(count, tp_size - 1),
+        sems(10),
+        sems(10),
+    ]
+    vmem = pl.BlockSpec(memory_space=pltpu.VMEM)
+    return pl.pallas_call(
+        functools.partial(reduce_kernel, specs, tp_size),
+        in_specs=[pl.BlockSpec(memory_space=pl.ANY)] * count + [vmem],
+        out_specs=[vmem] * (count + 2),
+        out_shape=[jax.ShapeDtypeStruct(spec.shard, f32) for spec in specs]
+        + [jax.ShapeDtypeStruct(small.shape, f32), jax.ShapeDtypeStruct((8, 128), f32)],
+        scratch_shapes=scratch,
+        compiler_params=pltpu.CompilerParams(
+            collective_id=2, has_side_effects=True, vmem_limit_bytes=60 << 20
+        ),
+        name="reduce_all",
+    )(*wholes, small)
+
+
 def bucket_onehot(offsets, buckets):
     offsets = jnp.maximum(offsets, 0)
     passed = jnp.sum((offsets[:, None] >= jnp.asarray(bucket_edges)).astype(jnp.int32), axis=-1)
@@ -183,11 +699,11 @@
     return grad_rows, jnp.sum(grad * scaled, axis=0)
 
 
-def ffn_kernel(x_ref, c_ref, wg_ref, wd_ref, out_ref, dx_ref, gg_ref, gd_ref):
+def ffn_kernel(x_ref, c_ref, wg_ref, wu_ref, wd_ref, out_ref, dx_ref, gg_ref, gu_ref, gd_ref):
     x = x_ref[...]
     c = c_ref[...]
-    wg = wg_ref[0, 0]
-    wu = wg_ref[0, 1]
+    wg = wg_ref[0]
+    wu = wu_ref[0]
     wd = wd_ref[...]
     gate = dotf(x, wg, ((1,), (0,)))
     upper = dotf(x, wu, ((1,), (0,)))
@@ -204,8 +720,8 @@
     part = dotf(hidden, wd, ((1,), (0,)))
     back = dotf(grad_gate, wg, ((1,), (1,))) + dotf(grad_upper, wu, ((1,), (1,)))
     gd_ref[...] = dotf(hidden, c, ((0,), (0,))).astype(bf16)
-    gg_ref[0, 0] = dotf(x, grad_gate, ((0,), (0,))).astype(bf16)
-    gg_ref[0, 1] = dotf(x, grad_upper, ((0,), (0,))).astype(bf16)
+    gg_ref[0] = dotf(x, grad_gate, ((0,), (0,))).astype(bf16)
+    gu_ref[0] = dotf(x, grad_upper, ((0,), (0,))).astype(bf16)
 
     @pl.when(pl.program_id(0) == 0)
     def _():
@@ -218,26 +734,27 @@
         dx_ref[...] += back
 
 
-def feed_forward(x, cot, w_gateup, w_down):
+def feed_forward(x, cot, w_gate, w_up, w_down):
     rows, width = x.shape
-    blocks, unused, unused_d, units = w_gateup.shape
+    blocks, unused, units = w_gate.shape
     whole = pl.BlockSpec((rows, width), lambda i: (0, 0))
-    gates = pl.BlockSpec((1, 2, width, units), lambda i: (i, 0, 0, 0))
+    gates = pl.BlockSpec((1, width, units), lambda i: (i, 0, 0))
     downs = pl.BlockSpec((units, width), lambda i: (i, 0))
     return pl.pallas_call(
         ffn_kernel,
         grid=(blocks,),
-        in_specs=[whole, whole, gates, downs],
-        out_specs=[whole, whole, gates, downs],
+        in_specs=[whole, whole, gates, gates, downs],
+        out_specs=[whole, whole, gates, gates, downs],
         out_shape=[
             jax.ShapeDtypeStruct((rows, width), f32),
             jax.ShapeDtypeStruct((rows, width), f32),
-            jax.ShapeDtypeStruct(w_gateup.shape, bf16),
+            jax.ShapeDtypeStruct(w_gate.shape, bf16),
+            jax.ShapeDtypeStruct(w_up.shape, bf16),
             jax.ShapeDtypeStruct(w_down.shape, bf16),
         ],
         compiler_params=pltpu.CompilerParams(vmem_limit_bytes=56 << 20),
         name="feed_forward",
-    )(x, cot, w_gateup, w_down)
+    )(x, cot, w_gate, w_up, w_down)
 
 
 def mm(a, b):
@@ -312,18 +829,74 @@
     rel_table_v,
 ):
     low = lambda w: w.astype(bf16)
-    w_query = gather_full(low(query_w), 0, 1)
-    w_keyval = gather_full(low(keyval_w), 1, 2)
-    w_out = gather_full(low(out_w), 1, 0)
-    w_cross_query = gather_full(low(cross_query_w), 0, 1)
-    w_cross_keyval = gather_full(low(cross_keyval_w), 1, 2)
-    w_cross_out = gather_full(low(cross_out_w), 1, 0)
-    w_gateup = gather_full(low(gateup_w)[None], 2, 0)
-    w_down = gather_full(low(down_w), 1, 0)
-    gain_low = lax.all_gather(low(gains), "dp", axis=1, tiled=True).astype(f32)
-    table_low = gather_full(low(rel_table), 1, 0)
-    rows_group = lax.all_gather(rows_in, "tp", axis=0, tiled=True)
-    memory_group = lax.all_gather(memory, "tp", axis=0, tiled=True)
+    tp_size = lax.axis_size("tp")
+    dp_size = lax.axis_size("dp")
+    here = dp_size == 8 and tp_size == 4
+    shards = [
+        low(query_w),
+        low(keyval_w),
+        low(out_w),
+        low(cross_query_w),
+        low(cross_keyval_w),
+        low(cross_out_w),
+        low(gateup_w[0]),
+        low(gateup_w[1]),
+        low(down_w),
+    ]
+    if here:
+        specs = [
+            Row((), *query_w.shape, tp_size),
+            Row((2,), *keyval_w.shape[1:], tp_size),
+            Column(out_w.shape[1], out_w.shape[0], tp_size),
+            Row((), *cross_query_w.shape, tp_size),
+            Row((2,), *cross_keyval_w.shape[1:], tp_size),
+            Column(cross_out_w.shape[1], cross_out_w.shape[0], tp_size),
+            Block(*gateup_w.shape[1:], tp_size),
+            Block(*gateup_w.shape[1:], tp_size),
+            Column(down_w.shape[1], down_w.shape[0], tp_size),
+        ]
+        misc = jnp.concatenate(
+            [
+                gains,
+                jnp.pad(rel_table, ((0, 0), (0, gains.shape[1] - rel_table.shape[1]))),
+                jnp.zeros((1, gains.shape[1]), f32),
+            ]
+        )
+        gathered = gather_all(
+            [misc] + shards + [rows_in, memory],
+            [Block(*misc.shape, tp_size)]
+            + specs
+            + [Rows(*rows_in.shape, tp_size), Rows(*memory.shape, tp_size)],
+            [True] * 10 + [False] * 2,
+            tp_size,
+        )
+        misc_all = gathered[0].reshape(tp_size, dp_size, *misc.shape)
+        gain_low = low(misc_all[0, :, :3].transpose(1, 0, 2).reshape(3, -1)).astype(f32)
+        table_low = low(
+            misc_all[:, :, 3:7, : rel_table.shape[1]].transpose(0, 2, 1, 3)
+        ).reshape(rel_table.shape[0] * tp_size, rel_table.shape[1] * dp_size)
+        weights = gathered[1:10]
+        rows_group, memory_group = gathered[10:]
+    else:
+        splits = ((0, 1), (1, 2), (1, 0), (0, 1), (1, 2), (1, 0), (1, 0), (1, 0), (1, 0))
+        shards[6] = shards[6][None]
+        shards[7] = shards[7][None]
+        weights = [gather_full(shard, *split) for shard, split in zip(shards, splits)]
+        gain_low = lax.all_gather(low(gains), "dp", axis=1, tiled=True).astype(f32)
+        table_low = gather_full(low(rel_table), 1, 0)
+        rows_group = lax.all_gather(rows_in, "tp", axis=0, tiled=True)
+        memory_group = lax.all_gather(memory, "tp", axis=0, tiled=True)
+    (
+        w_query,
+        w_keyval,
+        w_out,
+        w_cross_query,
+        w_cross_keyval,
+        w_cross_out,
+        w_gate,
+        w_up,
+        w_down,
+    ) = weights
 
     rows_local = rows_in.shape[0]
     key_rows = rows_group.shape[0]
@@ -358,8 +931,8 @@
     middle_two = middle + mm(cross_context, w_cross_out)
     normed_three = norm_rows(middle_two, gain_low[2])
 
-    hidden_out, grad_normed_three, grad_gateup, grad_down = feed_forward(
-        normed_three, cotangent, w_gateup, w_down
+    hidden_out, grad_normed_three, grad_gate, grad_up, grad_down = feed_forward(
+        normed_three, cotangent, w_gate, w_up, w_down
     )
     block_out = (middle_two + hidden_out).astype(bf16)
     back_three, grad_gain_three = norm_back(grad_normed_three, middle_two, gain_low[2])
@@ -416,21 +989,41 @@
     back_one, grad_gain_one = norm_back(grad_normed, residual, gain_low[0])
     grad_rows = grad_middle + back_one
 
-    reduced = (
-        scatter_sum(grad_query, 0, 1),
-        scatter_sum(grad_keyval, 1, 2),
-        scatter_sum(grad_out, 1, 0),
-        scatter_sum(grad_cross_query, 0, 1),
-        scatter_sum(grad_cross_keyval, 1, 2),
-        scatter_sum(grad_cross_out, 1, 0),
-        scatter_sum(grad_gateup, 2, 0)[0],
-        scatter_sum(grad_down, 1, 0),
-    )
-    squares = jnp.zeros((), f32)
-    for piece in reduced:
-        squares = squares + jnp.sum(piece * piece)
     gain_terms = jnp.stack([grad_gain_one, grad_gain_cross, grad_gain_three])
-    squares_all, gains_full, table_full = lax.psum((squares, gain_terms, grad_table), ("dp", "tp"))
+    wholes = [
+        grad_query,
+        grad_keyval,
+        grad_out,
+        grad_cross_query,
+        grad_cross_keyval,
+        grad_cross_out,
+        grad_gate,
+        grad_up,
+        grad_down,
+    ]
+    if here:
+        lanes = 128
+        small = jnp.concatenate(
+            [
+                gain_terms.reshape(-1, lanes),
+                jnp.pad(grad_table, ((0, 0), (0, lanes - grad_table.shape[1]))),
+            ]
+        )
+        *reduced, small_sum, square_rows = reduce_all(wholes, small, specs, tp_size)
+        gains_full = small_sum[: -grad_table.shape[0]].reshape(gain_terms.shape)
+        table_full = small_sum[-grad_table.shape[0] :, : grad_table.shape[1]]
+        squares_all = jnp.sum(square_rows[:, 0])
+    else:
+        reduced = [scatter_sum(whole, *split) for whole, split in zip(wholes, splits)]
+        reduced[6] = reduced[6][0]
+        reduced[7] = reduced[7][0]
+        squares = jnp.zeros((), f32)
+        for piece in reduced:
+            squares = squares + jnp.sum(piece * piece)
+        squares_all, gains_full, table_full = lax.psum(
+            (squares, gain_terms, grad_table), ("dp", "tp")
+        )
+    reduced = (*reduced[:6], jnp.stack([reduced[6], reduced[7]]), reduced[8])
     grad_norm = jnp.sqrt(
         squares_all + jnp.sum(gains_full * gains_full) + jnp.sum(table_full * table_full)
     )

time: 1250 us -> 530 us (0.42)
  waiting for transfers between devices: 800 us -> 20.8 us
  Pallas kernels: 76.4 us -> 387 us
  blocking collectives: 188 us -> 0 us
  local copies, waits for them, and re-layouts: 59.8 us -> 19.7 us
    reduce_scatter x10 -> x0, waiting for transfers between devices: 335 us -> none  [the longest x4 210 us: scatter_sum(): part = lax.psum_scatter(whole, 'dp', scatter_dimension=dp_axis, tiled=True)]
    pallas_call x0 -> x2, Pallas kernels: none -> 310 us  [the longest x1 165 us: reduce_all(): pl.pallas_call(functools.partial(reduce_kernel, specs, tp_size), in_specs...]
    all_gather x11 -> x0, waiting for transfers between devices: 228 us -> none  [the longest x8 202 us: gather_full(): return lax.all_gather(part, 'dp', axis=dp_axis, tiled=True)]
    unnamed x35 -> x2, waiting for transfers between devices: 227 us -> 0.03 us
    all_gather x10 -> x0, blocking collectives: 148 us -> none  [the longest x8 130 us: gather_full(): part = lax.all_gather(shard, 'tp', axis=tp_axis, tiled=True)]
    psum x1 -> x0, blocking collectives: 39.9 us -> none  [per_device(): lax.psum((squares, gain_terms, grad_table), ('dp', 'tp'))]
    unnamed x186 -> x181, local copies, waits for them, and re-layouts: 57.1 us -> 18.1 us
  transfers between devices with their start and end apart: 29 -> 2, of which waited for: 25 -> 1; matrix products, arithmetic and copies ran while one was open for 9% -> 5% of each run, Pallas kernels for 4% -> 4%
where the time goes in v2:
time: 530 us; the launch traced here: 522 us
  Pallas kernels  387 us (73%)
  other arithmetic  37.9 us (7%)
  matrix products  36.9 us (7%)
  waiting for transfers between devices  20.8 us (4%)
  between operations  20 us (4%)
  local copies, waits for them, and re-layouts  19.7 us (4%)
    pallas_call x1, Pallas kernels, reduce_all(): pl.pallas_call(functools.partial(reduce_kernel, specs, tp_size), in_specs...  165 us
    pallas_call x1, Pallas kernels, gather_all(): pl.pallas_call(functools.partial(gather_kernel, specs, plane, tp_size), i...  145 us
    pallas_call x2, Pallas kernels, attn_bwd(): pl.pallas_call(functools.partial(bwd_kernel, causal, groups), grid=(pairs...  29.9 us
    dot_general x17, matrix products, dotf(): return lax.dot_general(a, b, (dims, ((), ())), preferred_element_type=f32)  24.8 us
    pallas_call x2, Pallas kernels, attn_fwd(): pl.pallas_call(functools.partial(fwd_kernel, causal, groups), grid=(pairs...  24.7 us
    pallas_call x1, Pallas kernels, feed_forward(): pl.pallas_call(ffn_kernel, grid=(blocks,), in_specs=[whole, whole, gates,...  22.4 us
    reduce_scatter x1, waiting for transfers between devices, per_device(): lax.psum_scatter(jnp.concatenate([part_k, part_v], axis=1), 'tp', scatter...  20.8 us
    unnamed x181, local copies, waits for them, and re-layouts  18.1 us
  transfers between devices with their start and end apart: 2, of which 1 were waited for; matrix products, arithmetic and copies ran while one was open for 5% of the time, Pallas kernels for 4%

profile of v2, /device:TPU:0, one launch (start us, length us, event | category | flops | bytes accessed | tf_op | source)
XLA Modules:
  0.0 522.2 jit_solution(11295616951861878050)
XLA Ops:
  15.0 144.6 %gather_all.1 = (f32[4,64,128]{2,1,0:T(8,128)}, bf16[1024,1024]{1,0:T(8,128)(2,1)}, bf16[2,1024,512]{2,1,0:T(8,128)(2,1)}, bf16[1024,1024]{1,0:T(8,128)(2,1)}, b...) custom-call(f32[8,128]{1,0:T(8,128)} %fusion.65.refs_0_, ...), custom_call_target="tpu_custom_call" | custom-call | tf_op jit(solution)/shard_map/gather_all/pallas_call | solution.py:423
  160.7 2.1 fusion
  162.8 2.7 convolution_convert_fusion.8.v_ref
  172.2 2.3 convolution_convert_fusion.13.q_ref
  174.7 15.3 %attend_fwd.2 = (bf16[256,1024]{1,0:T(8,128)(2,1)S(1)}, bf16[16,256,1024]{2,1,0:T(8,128)(2,1)}) custom-call(s32[2]{0:T(128)S(1)} %get-tuple-element.269.scal_ref, bf16[256,1024]{1,0:T(8,128)(2,1)S(1)} %convolution_convert_fusion.13.q_ref, bf16[1024,512]{1,0:T(8,128)(2,1)S(1)} %convolution_convert_fusion.9.k_ref, ...), custom_call_target="tpu_custom_call" | custom-call | tf_op jit(solution)/shard_map/attend_fwd/pallas_call | solution.py:103
  192.6 9.4 %attend_fwd.3 = (bf16[256,1024]{1,0:T(8,128)(2,1)S(1)}, bf16[16,256,512]{2,1,0:T(8,128)(2,1)}) custom-call(s32[2]{0:T(128)S(1)} %get-tuple-element.270.scal_ref, bf16[256,1024]{1,0:T(8,128)(2,1)S(1)} %convolution_convert_fusion.12.q_ref, bf16[512,512]{1,0:T(8,128)(2,1)S(1)} %copy-done.3, bf16[512,512]{1,0:T(8,128)(2,1)S(1)} %copy-done.2), custom_call_target="tpu_custom_call" | custom-call | tf_op jit(solution)/shard_map/attend_fwd/pallas_call | solution.py:103
  203.7 22.4 %feed_forward.1 = (f32[256,1024]{1,0:T(8,128)}, f32[256,1024]{1,0:T(8,128)}, bf16[4,1024,704]{2,1,0:T(8,128)(2,1)}, bf16[4,1024,704]{2,1,0:T(8,128)(2,1)}, bf16[2816,1024]{1,0:T(8,128)(2,1)}) custom-call(bf16[256,1024]{1,0:T(8,128)(2,1)} %multiply_convert_fusion.x_ref, bf16[256,1024]{1,0:T(8,128)(2,1)} %c_ref.1, ...), custom_call_target="tpu_custom_call" | custom-call | tf_op jit(solution)/shard_map/feed_forward/pallas_call | solution.py:743
  227.9 2.5 multiply_add_fusion.1
  231.4 10.4 %attend_bwd.2 = (bf16[256,1024]{1,0:T(8,128)(2,1)S(1)}, bf16[512,512]{1,0:T(8,128)(2,1)S(1)}, bf16[512,512]{1,0:T(8,128)(2,1)S(1)}) custom-call(bf16[256,1024]{1,0:T(8,128)(2,1)S(1)} %convolution_convert_fusion.12.q_ref, bf16[512,512]{1,0:T(8,128)(2,1)S(1)} %copy-done.3, bf16[512,512]{1,0:T(8,128)(2,1)S(1)} %copy-done.2, ...), custom_call_target="tpu_custom_call" | custom-call | tf_op jit(solution)/shard_map/attend_bwd/pallas_call | solution.py:158
  243.8 3.1 multiply_reduce_fusion.1
  250.0 19.6 %attend_bwd.3 = (bf16[256,1024]{1,0:T(8,128)(2,1)S(1)}, bf16[1024,512]{1,0:T(8,128)(2,1)S(1)}, bf16[1024,512]{1,0:T(8,128)(2,1)S(1)}, f32[4,4,1280]{2,1,0:T(4,128)S(1)}) custom-call(bf16[256,1024]{1,0:T(8,128)(2,1)S(1)} %copy-done.5, bf16[1024,512]{1,0:T(8,128)(2,1)S(1)} %convolution_convert_fusion.9.k_ref, ...), custom_call_target="tpu_custom_call" | custom-call | tf_op jit(solution)/shard_map/attend_bwd/pallas_call | solution.py:158
  274.3 2.3 copy.98
  277.0 2.2 convolution_convert_fusion.3.refs_0_
  279.2 1.8 fusion.86
  281.0 2.1 convolution_convert_fusion.refs_5_
  283.1 2.1 convolution_convert_fusion.2.refs_2_
  285.2 2.2 convolution_convert_fusion.1.refs_3_
  294.3 20.8 %reduce-scatter.3.cloned.1.call-done = bf16[256,1024]{1,0:T(8,128)(2,1)} async-done(((bf16[1024,1024]{1,0:T(8,128)(2,1)}), bf16[256,1024]{1,0:T(8,128)(2,1)}) %reduce-scatter.3.cloned.1.call-update) | async-done | bytes 524304 | tf_op jit(solution)/shard_map/reduce_scatter | solution.py:971
  315.0 1.9 convolution_add_fusion.1
  317.1 2.1 fusion.16
  322.5 165.3 %reduce_all.1 = (f32[128,256]{1,0:T(8,128)}, f32[2,128,128]{2,1,0:T(8,128)}, f32[256,128]{1,0:T(8,128)}, f32[128,256]{1,0:T(8,128)}, f32[2,128,128]{2,1,0:T(8,12...) custom-call(bf16[1024,1024]{1,0:T(8,128)(2,1)} %convolution_convert_, ...), custom_call_target="tpu_custom_call" | custom-call | tf_op jit(solution)/shard_map/reduce_all/pallas_call | solution.py:665
  494.3 3.2 multiply_subtract_fusion
  497.5 2.4 copy.101
  499.9 2.3 copy.102
  (253 shorter events, 57.4 us)
Async XLA Ops:
  7.2 4.4 copy-start.47
  7.3 5.0 copy-start.45
  7.3 5.7 %copy-start.43 = (f32[2,128,128]{2,1,0:T(8,128)S(1)}, f32[2,128,128]{2,1,0:T(8,128)}, u32[]{:S(2)}) copy-start(f32[2,128,128]{2,1,0:T(8,128)} %param.46) | copy-start | bytes 393220
  7.3 280.1 %reduce-scatter.5.cloned.1.call-start = ((), (), s32[]{:S(2)}) async-start(), calls=%async_computation.3 | async-start | bytes 1310720 | tf_op jit(solution)/shard_map/reduce_scatter | solution.py:947
  8.8 150.8 %copy-start.25 = (f32[2,128,704]{2,1,0:T(8,128)}, f32[2,128,704]{2,1,0:T(8,128)S(1)}, u32[]{:S(2)}) copy-start(f32[2,128,704]{2,1,0:T(8,128)S(1)} %copy.93) | copy-start | bytes 2162692
  8.8 4.8 copy-start.42
  8.8 5.5 %copy-start.77 = (f32[3,128]{1,0:T(4,128)S(1)}, f32[3,128]{1,0:T(4,128)}, u32[]{:S(2)}) copy-start(f32[3,128]{1,0:T(4,128)} %param.50) | copy-start | bytes 4612
  8.8 5.5 %copy-start.79 = (f32[4,4]{1,0:T(4,128)S(1)}, f32[4,4]{1,0:T(4,128)}, u32[]{:S(2)}) copy-start(f32[4,4]{1,0:T(4,128)} %param.51) | copy-start | bytes 196
  174.6 16.2 %copy-start.4 = (bf16[256,1024]{1,0:T(8,128)(2,1)}, bf16[256,1024]{1,0:T(8,128)(2,1)S(1)}, u32[]{:S(2)}) copy-start(bf16[256,1024]{1,0:T(8,128)(2,1)S(1)} %convolution_convert_fusion.13.q_ref) | copy-start | bytes 1572868
  174.6 15.4 %copy-start.20 = (bf16[1024,1024]{1,0:T(8,128)(2,1)S(1)}, bf16[1024,1024]{1,0:T(8,128)(2,1)}, u32[]{:S(2)}) copy-start(bf16[1024,1024]{1,0:T(8,128)(2,1)} %get-tuple-element.78) | copy-start | bytes 6291460
  190.8 11.1 %copy-start.9 = (f32[256,1024]{1,0:T(8,128)}, f32[256,1024]{1,0:T(8,128)S(1)}, u32[]{:S(2)}) copy-start(f32[256,1024]{1,0:T(8,128)S(1)} %get-tuple-element.264) | copy-start | bytes 3145732
  191.6 10.4 %copy-start.22 = (bf16[1024,1024]{1,0:T(8,128)(2,1)S(1)}, bf16[1024,1024]{1,0:T(8,128)(2,1)}, u32[]{:S(2)}) copy-start(bf16[1024,1024]{1,0:T(8,128)(2,1)} %get-tuple-element.83) | copy-start | bytes 6291460
  243.7 71.3 %reduce-scatter.3.cloned.1.call-start = ((), (), s32[]{:S(2)}) async-start(), calls=%async_computation.2 | async-start | bytes 2621440 | tf_op jit(solution)/shard_map/reduce_scatter | solution.py:971
  272.1 5.0 copy-start.7
  272.1 5.0 copy-start.18
  292.5 22.5 %copy-start.27 = (f32[256,1024]{1,0:T(8,128)S(1)}, f32[256,1024]{1,0:T(8,128)}, u32[]{:S(2)}) copy-start(f32[256,1024]{1,0:T(8,128)} %fusion.86) | copy-start | bytes 3145732
  294.3 22.7 %copy-start.19 = (bf16[256,1024]{1,0:T(8,128)(2,1)S(1)}, bf16[256,1024]{1,0:T(8,128)(2,1)}, u32[]{:S(2)}) copy-start(bf16[256,1024]{1,0:T(8,128)(2,1)} %refs_10_.1) | copy-start | bytes 1572868
  322.5 171.8 %copy-start.26 = (f32[2,128,704]{2,1,0:T(8,128)S(1)}, f32[2,128,704]{2,1,0:T(8,128)}, u32[]{:S(2)}) copy-start(f32[2,128,704]{2,1,0:T(8,128)} %copy-done.25) | copy-start | bytes 2162692
  322.5 171.8 %copy-start.29 = (f32[2,128,704]{2,1,0:T(8,128)S(1)}, f32[2,128,704]{2,1,0:T(8,128)}, u32[]{:S(2)}) copy-start(f32[2,128,704]{2,1,0:T(8,128)} %copy.97) | copy-start | bytes 2162692
  497.5 4.7 copy-start.30
  497.5 6.6 %copy-start.39 = (f32[256,1024]{1,0:T(8,128)S(1)}, f32[256,1024]{1,0:T(8,128)}, u32[]{:S(2)}) copy-start(f32[256,1024]{1,0:T(8,128)} %get-tuple-element.268) | copy-start | bytes 3145732
  507.7 5.4 %copy-start.80 = (f32[4,4]{1,0:T(4,128)S(1)}, f32[4,4]{1,0:T(4,128)}, u32[]{:S(2)}) copy-start(f32[4,4]{1,0:T(4,128)} %param.51) | copy-start | bytes 196
  507.7 5.4 %copy-start.83 = (f32[4,4]{1,0:T(4,128)S(1)}, f32[4,4]{1,0:T(4,128)}, u32[]{:S(2)}) copy-start(f32[4,4]{1,0:T(4,128)} %param.71) | copy-start | bytes 196
  507.7 5.4 %copy-start.84 = (f32[4,4]{1,0:T(4,128)S(1)}, f32[4,4]{1,0:T(4,128)}, u32[]{:S(2)}) copy-start(f32[4,4]{1,0:T(4,128)} %param.61) | copy-start | bytes 196
  (65 other events, 163.7 us)
Sparse Core Ops, SparseCore 0:
  243.8 26.0 reduce-scatter.4
  272.3 42.7 reduce-scatter.2
